TPU v7x, 128 devices: a whole 4x4x4 slice. The times are simulated.
128 devices in a mesh: spatial: 8 (over z, core), filter: 8 (over y, x_lo), sample: 2 (over x_hi).
Axes of the slice: x: 4 (x_hi: 2, x_lo: 2; x = x_hi * 2 + x_lo), y: 4, z: 4, core: 2. Of those that a mesh axis runs over, the one named last changes fastest.
Arguments:
- volume: bfloat16 [2, 64, 32, 16, 128], P('sample', None, 'spatial', 'filter'), may hold values from -6 to 6
- weight_first: bfloat16 [27, 64, 128], replicated, may hold values from -0.15625 to 0.15625
- weight_second: bfloat16 [27, 128, 256], P(None, None, 'filter'), may hold values from -0.109375 to 0.109375
- cotangent: bfloat16 [2, 256, 32, 16, 128], P('sample', 'filter', 'spatial'), may hold values from -6 to 6
Outputs:
- mapped: float32 [2, 256, 32, 16, 128], P('sample', 'filter', 'spatial')
- second_grad: float32 [27, 128, 256], P(None, None, 'filter')
- first_grad: float32 [27, 64, 128], replicated
- volume_grad: float32 [2, 64, 32, 16, 128], P('sample', None, 'spatial', 'filter')
All inputs are finite; a program needn't handle non-finite values.
Results may differ from a plain program's by a relative error of at most 0.003.
Values may be sent and summed in bfloat16 or wider, within the bound.
A program may use at most 256 MiB of HBM per device.

v0:
```python
import math

import jax
import jax.numpy as jnp
from jax import lax
from jax.sharding import PartitionSpec as P


def extended_2(cells, sides, width):
    for axis, dim in sides:
        count = lax.axis_size(axis)
        ends = count - 1
        head = lax.slice_in_dim(cells, 0, width, axis=dim)
        tail = lax.slice_in_dim(cells, cells.shape[dim] - width, cells.shape[dim], axis=dim)
        cells = jnp.concatenate(
            [
                lax.ppermute(tail, axis, [(i, (i + 1) % count) for i in range(ends)]),
                cells,
                lax.ppermute(head, axis, [((i + 1) % count, i) for i in range(ends)]),
            ],
            axis=dim,
        )
    return cells


def pad_third(field):
    return jnp.pad(field, ((0, 0), (0, 0), (0, 0), (0, 0), (1, 1)))


def pad_second_third(field):
    return jnp.pad(field, ((0, 0), (0, 0), (0, 0), (1, 1), (1, 1)))


def forward_terms(padded, weight, depth, height, length):
    total = None
    for step_x in range(3):
        for step_y in range(3):
            for step_z in range(3):
                offset = step_x * 9 + step_y * 3 + step_z
                piece = padded[
                    :,
                    :,
                    step_x : step_x + depth,
                    step_y : step_y + height,
                    step_z : step_z + length,
                ]
                term = jnp.einsum(
                    "io,sixyz->soxyz", weight[offset], piece, preferred_element_type=jnp.float32
                )
                total = term if total is None else total + term
    return total


def backward_terms(padded, weight, depth, height, length):
    total = None
    for step_x in range(3):
        for step_y in range(3):
            for step_z in range(3):
                offset = step_x * 9 + step_y * 3 + step_z
                piece = padded[
                    :,
                    :,
                    2 - step_x : 2 - step_x + depth,
                    2 - step_y : 2 - step_y + height,
                    2 - step_z : 2 - step_z + length,
                ]
                term = jnp.einsum(
                    "io,soxyz->sixyz", weight[offset], piece, preferred_element_type=jnp.float32
                )
                total = term if total is None else total + term
    return total


def weight_terms(padded, grads, depth, height, length):
    terms = []
    for step_x in range(3):
        for step_y in range(3):
            for step_z in range(3):
                piece = padded[
                    :,
                    :,
                    step_x : step_x + depth,
                    step_y : step_y + height,
                    step_z : step_z + length,
                ]
                terms.append(
                    jnp.einsum("sixyz,soxyz->io", piece, grads, preferred_element_type=jnp.float32)
                )
    return jnp.stack(terms)


def on_device(volume, weight_first, weight_second, cotangent):
    count, _, depth, height, length = volume.shape
    filters = lax.axis_size("filter")
    total_cells = (
        lax.axis_size("sample")
        * count
        * depth
        * lax.axis_size("spatial")
        * height
        * filters
        * length
    )
    scaling = 1.0 / math.sqrt(total_cells)
    vol_padded = pad_third(extended_2(volume, (("spatial", 2), ("filter", 3)), 1))
    first_pre = forward_terms(vol_padded, weight_first, depth, height, length)
    hidden = jax.nn.silu(first_pre).astype(jnp.bfloat16)
    whole = lax.all_gather(hidden, "filter", axis=3, tiled=True)
    extended = pad_second_third(extended_2(whole, (("spatial", 2),), 1))
    mapped = forward_terms(extended, weight_second, depth, height * filters, length)
    cot_padded = pad_second_third(extended_2(cotangent, (("spatial", 2),), 1))
    partial_grad = backward_terms(cot_padded, weight_second, depth, height * filters, length)
    back_hidden = lax.psum_scatter(partial_grad, "filter", scatter_dimension=3, tiled=True)
    second_local = weight_terms(extended, cotangent, depth, height * filters, length)
    second_grad = lax.psum(second_local, ("spatial", "sample")) * scaling
    sigmoid_value = jax.nn.sigmoid(first_pre)
    back_pre = (back_hidden * (sigmoid_value * (1.0 + first_pre * (1.0 - sigmoid_value)))).astype(
        jnp.bfloat16
    )
    grad_padded = pad_third(extended_2(back_pre, (("spatial", 2), ("filter", 3)), 1))
    volume_grad = backward_terms(grad_padded, weight_first, depth, height, length)
    first_local = weight_terms(vol_padded, back_pre, depth, height, length)
    first_grad = lax.psum(first_local, ("spatial", "filter", "sample")) * scaling
    return (mapped, second_grad, first_grad, volume_grad)


def solution(mesh):
    placed = (
        P("sample", None, "spatial", "filter", None),
        P(),
        P(None, None, "filter"),
        P("sample", "filter", "spatial", None, None),
    )
    return jax.shard_map(
        on_device,
        mesh=mesh,
        in_specs=placed,
        out_specs=(
            P("sample", "filter", "spatial", None, None),
            P(None, None, "filter"),
            P(),
            P("sample", None, "spatial", "filter", None),
        ),
        check_vma=False,
    )
```

profile of v0, /device:TPU:1, one launch (start us, length us, event | category | flops | bytes accessed | tf_op | source)
XLA Modules:
  0.0 792.1 jit_solution(15124438737630124006)
XLA Ops:
  8.7 4.9 collective-permute-start.6
  16.5 3.6 collective-permute-start
  22.1 3.8 fusion.454
  27.3 3.1 collective-permute-start.2
  36.9 3.1 fusion.233
  40.0 3.1 fusion.234
  45.8 3.0 fusion.239
  48.8 2.8 fusion.240
  51.6 3.1 fusion.241
  54.7 3.0 fusion.242
  57.7 2.9 fusion.243
  60.6 3.0 fusion.244
  63.6 3.0 fusion.245
  69.4 3.1 fusion.247
  75.3 3.0 fusion.249
  78.3 3.5 fusion.250
  84.6 3.0 fusion.252
  87.6 3.2 fusion.253
  93.5 3.1 fusion.259
  99.3 3.0 fusion.261
  102.3 3.1 fusion.262
  116.9 35.7 %bitcast_add_fusion = f32[1,128,4,16,128]{1,4,3,2,0:T(8,128)} fusion(f32[4,16,128,128]{3,2,1,0:T(8,128)} %fusion.232, f32[4,16,128,128]{3,2,1,0:T(8,128)} %fusion.233, f32[4,16,128,128]{3,2,1,0:T(8,128)} %fusion.234, f32[4,16,128,128]{3,2,1,0:T(8,128)} %fusion.235, f32[4,16,128,128]{3,2,1,0:T(8,128)} %fusion.239, f32[4,16,128,128]{3,2,1,0:T(8,128)} %fusion.240, ...), kind=kOutput, calls=%fused_computation.11 | convolution fusion | flops 94633984 | bytes 113909760 | tf_op jit(solution)/shard_map/io,soxyz->sixyz/dot_general | solution.py:67
  176.4 163.2 %all-reduce.13.cloned.1.call-done = f32[1,128,4,16,128]{1,4,3,2,0:T(8,128)} async-done(((f32[1,128,4,16,128]{1,4,3,2,0:T(8,128)}), f32[1,128,4,16,128]{1,4,3,2,0:T(8,128)}) %all-reduce.13.cloned.1.call-update) | async-done | bytes 4194320
  339.6 3.6 fusion.263
  343.4 4.0 collective-permute-start.8
  359.9 11.3 %collective-permute-done.11 = bf16[1,128,6,1,128]{1,4,3,2,0:T(8,128)(2,1)S(1)} collective-permute-done((bf16[1,128,6,1,128]{1,4,3,2,0:T(8,128)(2,1)S(1)}, bf16[1,128,6,1,128]{1,4,3,2,0:T(8,128)(2,1)S(1)}, u32[]{:S(2)}, u32[]{:S(2)}) %collective-permute-start.11) | collective-permute-done | bytes 196640 | tf_op jit(solution)/shard_map/ppermute | solution.py:19
  378.2 27.6 %all-gather.2.cloned.1.call-done = bf16[1,128,4,16,128]{1,4,3,2,0:T(8,128)(2,1)} async-done(((bf16[1,128,4,2,128]{1,4,3,2,0:T(8,128)(2,1)}), bf16[1,128,4,16,128]{1,4,3,2,0:T(8,128)(2,1)}) %all-gather.2.cloned.1.call-update) | async-done | bytes 2097168 | tf_op jit(solution)/shard_map/all_gather | solution.py:108
  408.3 5.0 collective-permute-start.4
  415.2 144.2 %all-reduce.11.cloned.1.call-done = f32[27,64,128]{2,1,0:T(8,128)} async-done(((f32[27,64,128]{2,1,0:T(8,128)}), f32[27,64,128]{2,1,0:T(8,128)}) %all-reduce.11.cloned.1.call-update) | async-done | bytes 884752 | tf_op jit(solution)/shard_map/psum | solution.py:123
  562.5 4.2 select_maximum_fusion
  648.0 5.4 fusion.100
  659.8 123.8 %all-reduce.9.cloned.1.call-done = f32[27,128,32]{1,2,0:T(8,128)} async-done(((f32[27,128,32]{1,2,0:T(8,128)}), f32[27,128,32]{1,2,0:T(8,128)}) %all-reduce.9.cloned.1.call-update) | async-done | bytes 442384 | tf_op jit(solution)/shard_map/psum | solution.py:115
  (246 shorter events, 180.5 us)
Async XLA Ops:
  7.2 18.8 %copy-start.28 = (u32[128]{0:T(128)S(1)}, u32[128]{0:T(128)}, u32[]{:S(2)}) copy-start(u32[128]{0:T(128)} %constant.22) | copy-start | bytes 1540
  7.2 20.0 %copy-start.11 = (bf16[1,64,4,2,128]{4,3,2,1,0:T(2,128)(2,1)S(1)}, bf16[1,64,4,2,128]{4,3,2,1,0:T(2,128)(2,1)}, u32[]{:S(2)}) copy-start(bf16[1,64,4,2,128]{4,3,2,1,0:T(2,128)(2,1)} %param.4) | copy-start | bytes 393220
  7.2 332.4 %all-reduce.13.cloned.1.call-start = ((), (), s32[]{:S(2)}) async-start(), calls=%async_computation.3 | async-start | bytes 8388608
  8.7 24.0 %collective-permute-start.6 = (bf16[1,32,1,16,128]{4,1,3,2,0:T(8,128)(2,1)S(1)}, bf16[1,32,1,16,128]{4,1,3,2,0:T(8,128)(2,1)S(1)}, u32[]{:S(2)}, u32[]{:S(2)}) collective-permute-start(bf16[1,32,1,16,128]{4,1,3,2,0:T(8,128)(2,1)S(1)} %get-tuple-element.16), channel_id=1, source_target_pairs={{0,16},{16,32},{32,48},{48,64},{64,80},{80,96},{96,112},{1,17},{17... | collective-permute-start | bytes 393224 | tf_op jit(solution)/shard_map/ppermute | solution.py:17
  13.6 19.1 %collective-permute-start.7 = (bf16[1,32,1,16,128]{4,1,3,2,0:T(8,128)(2,1)S(1)}, bf16[1,32,1,16,128]{4,1,3,2,0:T(8,128)(2,1)S(1)}, u32[]{:S(2)}, u32[]{:S(2)}) collective-permute-start(bf16[1,32,1,16,128]{4,1,3,2,0:T(8,128)(2,1)S(1)} %get-tuple-element.17), channel_id=1, source_target_pairs={{16,0},{32,16},{48,32},{64,48},{80,64},{96,80},{112,96},{17,1},{33... | collective-permute-start | bytes 393224 | tf_op jit(solution)/shard_map/ppermute | solution.py:19
  16.5 10.7 %collective-permute-start = (bf16[1,64,1,2,128]{4,1,3,2,0:T(8,128)(2,1)S(1)}, bf16[1,64,1,2,128]{4,1,3,2,0:T(8,128)(2,1)S(1)}, u32[]{:S(2)}, u32[]{:S(2)}) collective-permute-start(bf16[1,64,1,2,128]{4,1,3,2,0:T(8,128)(2,1)S(1)} %get-tuple-element.27), channel_id=1, source_target_pairs={{0,16},{16,32},{32,48},{48,64},{64,80},{80,96},{96,112},{1,17},{17... | collective-permute-start | bytes 98312 | tf_op jit(solution)/shard_map/ppermute | solution.py:17
  20.1 7.1 collective-permute-start.1
  22.1 12.1 %copy-start.21 = (bf16[27,128,32]{1,2,0:T(8,128)(2,1)S(1)}, bf16[27,128,32]{1,2,0:T(8,128)(2,1)}, u32[]{:S(2)}) copy-start(bf16[27,128,32]{1,2,0:T(8,128)(2,1)} %param.6) | copy-start | bytes 663556
  27.2 9.6 %copy-start.23 = (bf16[1,64,1,2,128]{4,1,3,2,0:T(8,128)(2,1)}, bf16[1,64,1,2,128]{4,1,3,2,0:T(8,128)(2,1)S(1)}, u32[]{:S(2)}) copy-start(bf16[1,64,1,2,128]{4,1,3,2,0:T(8,128)(2,1)S(1)} %collective-permute-done.1) | copy-start | bytes 98308
  27.3 78.1 %collective-permute-start.2 = (bf16[1,64,6,1,128]{4,1,3,2,0:T(8,128)(2,1)S(1)}, bf16[1,64,6,1,128]{4,1,3,2,0:T(8,128)(2,1)S(1)}, u32[]{:S(2)}, u32[]{:S(2)}) collective-permute-start(bf16[1,64,6,1,128]{4,1,3,2,0:T(8,128)(2,1)S(1)} %get-tuple-element.24), channel_id=1, source_target_pairs={{0,2},{2,4},{4,6},{6,8},{8,10},{10,12},{12,14},{1,3},{3,5},{5,7},{... | collective-permute-start | bytes 294920 | tf_op jit(solution)/shard_map/ppermute | solution.py:17
  30.4 75.0 %collective-permute-start.3 = (bf16[1,64,6,1,128]{4,1,3,2,0:T(8,128)(2,1)S(1)}, bf16[1,64,6,1,128]{4,1,3,2,0:T(8,128)(2,1)S(1)}, u32[]{:S(2)}, u32[]{:S(2)}) collective-permute-start(bf16[1,64,6,1,128]{4,1,3,2,0:T(8,128)(2,1)S(1)} %get-tuple-element.25), channel_id=1, source_target_pairs={{2,0},{4,2},{6,4},{8,6},{10,8},{12,10},{14,12},{3,1},{5,3},{7,5},{... | collective-permute-start | bytes 294920 | tf_op jit(solution)/shard_map/ppermute | solution.py:19
  152.7 253.2 %all-gather.2.cloned.1.call-start = ((), (), s32[]{:S(2)}) async-start(), calls=%async_computation | async-start | bytes 2359296 | tf_op jit(solution)/shard_map/all_gather | solution.py:108
  154.7 10.5 %copy-start.26 = (bf16[1,64,1,2,128]{4,1,3,2,0:T(8,128)(2,1)S(1)}, bf16[1,64,1,2,128]{4,1,3,2,0:T(8,128)(2,1)}, u32[]{:S(2)}) copy-start(bf16[1,64,1,2,128]{4,1,3,2,0:T(8,128)(2,1)} %copy-done.25) | copy-start | bytes 98308
  176.4 173.6 %copy-start.27 = (bf16[1,64,1,2,128]{4,1,3,2,0:T(8,128)(2,1)S(1)}, bf16[1,64,1,2,128]{4,1,3,2,0:T(8,128)(2,1)}, u32[]{:S(2)}) copy-start(bf16[1,64,1,2,128]{4,1,3,2,0:T(8,128)(2,1)} %copy-done.25) | copy-start | bytes 98308
  343.4 11.0 %collective-permute-start.8 = (bf16[1,128,1,2,128]{1,4,3,2,0:T(8,128)(2,1)S(1)}, bf16[1,128,1,2,128]{1,4,3,2,0:T(8,128)(2,1)S(1)}, u32[]{:S(2)}, u32[]{:S(2)}) collective-permute-start(bf16[1,128,1,2,128]{1,4,3,2,0:T(8,128)(2,1)S(1)} %get-tuple-element.22), channel_id=1, source_target_pairs={{0,16},{16,32},{32,48},{48,64},{64,80},{80,96},{96,112},{1,17},{17... | collective-permute-start | bytes 196616 | tf_op jit(solution)/shard_map/ppermute | solution.py:17
  347.4 7.1 collective-permute-start.9
  351.6 207.8 %all-reduce.11.cloned.1.call-start = ((), (), s32[]{:S(2)}) async-start(), calls=%async_computation.2 | async-start | bytes 1769472 | tf_op jit(solution)/shard_map/psum | solution.py:123
  354.5 5.3 collective-permute-start.10
  356.7 14.5 %collective-permute-start.11 = (bf16[1,128,6,1,128]{1,4,3,2,0:T(8,128)(2,1)S(1)}, bf16[1,128,6,1,128]{1,4,3,2,0:T(8,128)(2,1)S(1)}, u32[]{:S(2)}, u32[]{:S(2)}) collective-permute-start(bf16[1,128,6,1,128]{1,4,3,2,0:T(8,128)(2,1)S(1)} %get-tuple-element.21), channel_id=1, source_target_pairs={{2,0},{4,2},{6,4},{8,6},{10,8},{12,10},{14,12},{3,1},{5,3},{7,5},{... | collective-permute-start | bytes 589832 | tf_op jit(solution)/shard_map/ppermute | solution.py:19
  359.1 424.4 %all-reduce.9.cloned.1.call-start = ((), (), s32[]{:S(2)}) async-start(), calls=%async_computation.1 | async-start | bytes 884736 | tf_op jit(solution)/shard_map/psum | solution.py:115
  376.9 184.7 %copy-start.22 = (bf16[27,128,32]{1,2,0:T(8,128)(2,1)S(1)}, bf16[27,128,32]{1,2,0:T(8,128)(2,1)}, u32[]{:S(2)}) copy-start(bf16[27,128,32]{1,2,0:T(8,128)(2,1)} %param.6) | copy-start | bytes 663556
  405.9 155.8 %copy-start.2 = (bf16[1,128,4,16,128]{1,4,3,2,0:T(8,128)(2,1)S(1)}, bf16[1,128,4,16,128]{1,4,3,2,0:T(8,128)(2,1)}, u32[]{:S(2)}) copy-start(bf16[1,128,4,16,128]{1,4,3,2,0:T(8,128)(2,1)} %all-gather.2.cloned.1.call-done) | copy-start | bytes 6291460
  408.3 154.2 %collective-permute-start.4 = (bf16[1,128,1,16,128]{1,4,3,2,0:T(8,128)(2,1)}, bf16[1,128,1,16,128]{1,4,3,2,0:T(8,128)(2,1)}, u32[]{:S(2)}, u32[]{:S(2)}) collective-permute-start(bf16[1,128,1,16,128]{1,4,3,2,0:T(8,128)(2,1)} %get-tuple-element.12), channel_id=1, source_target_pairs={{0,16},{16,32},{32,48},{48,64},{64,80},{80,96},{96,112},{1,17},{17... | collective-permute-start | bytes 1572872 | tf_op jit(solution)/shard_map/ppermute | solution.py:17
  413.3 149.2 %collective-permute-start.5 = (bf16[1,128,1,16,128]{1,4,3,2,0:T(8,128)(2,1)}, bf16[1,128,1,16,128]{1,4,3,2,0:T(8,128)(2,1)}, u32[]{:S(2)}, u32[]{:S(2)}) collective-permute-start(bf16[1,128,1,16,128]{1,4,3,2,0:T(8,128)(2,1)} %get-tuple-element.13), channel_id=1, source_target_pairs={{16,0},{32,16},{48,32},{64,48},{80,64},{96,80},{112,96},{17,1},{33... | collective-permute-start | bytes 1572872 | tf_op jit(solution)/shard_map/ppermute | solution.py:19
  566.7 77.7 %copy-start = (bf16[1,128,6,18,130]{1,4,3,2,0:T(8,128)(2,1)}, bf16[1,128,6,18,130]{1,4,3,2,0:T(8,128)(2,1)S(1)}, u32[]{:S(2)}) copy-start(bf16[1,128,6,18,130]{1,4,3,2,0:T(8,128)(2,1)S(1)} %select_maximum_fusion) | copy-start | bytes 10782724
  647.9 8.2 %copy-start.7 = (f32[1,32,4,16,128]{4,1,3,2,0:T(8,128)S(1)}, f32[1,32,4,16,128]{4,1,3,2,0:T(8,128)}, u32[]{:S(2)}) copy-start(f32[1,32,4,16,128]{4,1,3,2,0:T(8,128)} %fusion.75) | copy-start | bytes 3145732
  648.0 8.2 %copy-start.13 = (f32[1,32,4,16,128]{4,1,3,2,0:T(8,128)S(1)}, f32[1,32,4,16,128]{4,1,3,2,0:T(8,128)}, u32[]{:S(2)}) copy-start(f32[1,32,4,16,128]{4,1,3,2,0:T(8,128)} %fusion.68) | copy-start | bytes 3145732
  648.0 8.2 %copy-start.14 = (f32[1,32,4,16,128]{4,1,3,2,0:T(8,128)S(1)}, f32[1,32,4,16,128]{4,1,3,2,0:T(8,128)}, u32[]{:S(2)}) copy-start(f32[1,32,4,16,128]{4,1,3,2,0:T(8,128)} %fusion.69) | copy-start | bytes 3145732
  648.0 8.2 %copy-start.15 = (f32[1,32,4,16,128]{4,1,3,2,0:T(8,128)S(1)}, f32[1,32,4,16,128]{4,1,3,2,0:T(8,128)}, u32[]{:S(2)}) copy-start(f32[1,32,4,16,128]{4,1,3,2,0:T(8,128)} %fusion.71) | copy-start | bytes 3145732
  648.0 8.2 %copy-start.16 = (f32[1,32,4,16,128]{4,1,3,2,0:T(8,128)S(1)}, f32[1,32,4,16,128]{4,1,3,2,0:T(8,128)}, u32[]{:S(2)}) copy-start(f32[1,32,4,16,128]{4,1,3,2,0:T(8,128)} %fusion.73) | copy-start | bytes 3145732
  648.0 8.2 %copy-start.17 = (f32[1,32,4,16,128]{4,1,3,2,0:T(8,128)S(1)}, f32[1,32,4,16,128]{4,1,3,2,0:T(8,128)}, u32[]{:S(2)}) copy-start(f32[1,32,4,16,128]{4,1,3,2,0:T(8,128)} %fusion.74) | copy-start | bytes 3145732
  648.0 8.2 %copy-start.18 = (f32[1,32,4,16,128]{4,1,3,2,0:T(8,128)S(1)}, f32[1,32,4,16,128]{4,1,3,2,0:T(8,128)}, u32[]{:S(2)}) copy-start(f32[1,32,4,16,128]{4,1,3,2,0:T(8,128)} %fusion.76) | copy-start | bytes 3145732
  (13 other events, 49.8 us)
Sparse Core Ops, SparseCore 0:
  152.8 186.7 all-reduce.12
  351.7 54.1 all-gather.1
  411.2 148.1 all-reduce.10
  646.0 137.5 all-reduce.8
where the time goes:
time: 797 us; the launch traced here: 792 us
  waiting for transfers between devices  471 us (59%)
  matrix products  252 us (32%)
  starting transfers between devices  33.4 us (4%)
  between operations  15.8 us (2%)
  other arithmetic  10.4 us (1%)
  local copies, waits for them, and re-layouts  9.52 us (1%)
    unnamed x5, waiting for transfers between devices  163 us
    psum x1, waiting for transfers between devices, on_device(): lax.psum(first_local, ('spatial', 'filter', 'sample')) * scaling  144 us
    psum x1, waiting for transfers between devices, on_device(): second_grad = lax.psum(second_local, ('spatial', 'sample')) * scaling  124 us
    dot_general x54, matrix products, backward_terms(): jnp.einsum('io,soxyz->sixyz', weight[offset], piece, preferred_element_ty...  119 us
    dot_general x54, matrix products, forward_terms(): jnp.einsum('io,sixyz->soxyz', weight[offset], piece, preferred_element_ty...  88.6 us
    dot_general x54, matrix products, weight_terms(): jnp.einsum('sixyz,soxyz->io', piece, grads, preferred_element_type=jnp.fl...  44.3 us
    all_gather x1, waiting for transfers between devices, on_device(): whole = lax.all_gather(hidden, 'filter', axis=3, tiled=True)  27.6 us
    ppermute x6, starting transfers between devices, extended_2(): lax.ppermute(tail, axis, [(i, (i + 1) % count) for i in range(ends)])  22.8 us
  transfers between devices with their start and end apart: 16, of which 6 were waited for; matrix products, arithmetic and copies ran while one was open for 17% of the time, Pallas kernels for 0%

commit v1 on v0

v1 whole, which is shorter than its diff:
```python
import functools
import math

import jax
import jax.numpy as jnp
from jax import lax
from jax.experimental import pallas as pl
from jax.experimental.pallas import tpu as pltpu
from jax.sharding import PartitionSpec as P

MESH = pl.DeviceIdType.MESH
BF = jnp.bfloat16
F32 = jnp.float32
VMEM = pl.BlockSpec(memory_space=pltpu.VMEM)
LIMIT = 56 * 1024 * 1024


def remote(src, dst, send, recv, device):
    return pltpu.make_async_remote_copy(
        src_ref=src, dst_ref=dst, send_sem=send, recv_sem=recv, device_id=device, device_id_type=MESH
    )


def greet(partners):
    barrier = pltpu.get_barrier_semaphore()
    for partner in partners:
        pl.semaphore_signal(barrier, inc=1, device_id=partner, device_id_type=MESH)
    pl.semaphore_wait(barrier, len(partners))


def places():
    ns, nf, nm = lax.axis_size("spatial"), lax.axis_size("filter"), lax.axis_size("sample")
    s, f, m = lax.axis_index("spatial"), lax.axis_index("filter"), lax.axis_index("sample")
    return ns, nf, nm, s, f, m


def call(kernel, count, outs, scratch, collective_id=None):
    params = dict(vmem_limit_bytes=LIMIT)
    if collective_id is not None:
        params.update(collective_id=collective_id, has_side_effects=True)
    return pl.pallas_call(
        kernel,
        out_shape=[jax.ShapeDtypeStruct(shape, dtype) for shape, dtype in outs],
        in_specs=[VMEM] * count,
        out_specs=[VMEM] * len(outs),
        scratch_shapes=scratch,
        compiler_params=pltpu.CompilerParams(**params),
    )


def dma(n):
    return pltpu.SemaphoreType.DMA((n,))


def exchange_inputs(
    vt, ct, wl, vs, cx, cg, wg,
    v_s, v_r, c_s, c_r, h_s, h_r, e_s, e_r, w_s, w_r, x_s, x_r, y_s, y_r, q_s, q_r,
):
    ns, nf, nm, s, f, m = places()
    depth = vt.shape[0]
    rows = 2 * nf
    part = wl.shape[0] // ns
    nz = ns // 2
    core, z = lax.rem(s, 2), s // 2
    prev, after = {"spatial": lax.rem(s + ns - 1, ns)}, {"spatial": lax.rem(s + 1, ns)}
    peers = [lax.rem(f + r, nf) for r in range(1, nf)]
    greet([{"filter": p} for p in peers] + [{"spatial": lax.rem(s + r, ns)} for r in range(1, ns)])

    halo = [
        remote(ct.at[0], cx.at[depth + 1], h_s.at[0], h_r.at[0], prev),
        remote(ct.at[depth - 1], cx.at[0], h_s.at[1], h_r.at[1], after),
    ]
    for copy in halo:
        copy.start()
    mine = pl.ds(s * part, part)
    weights = [
        remote(wl.at[mine], wg.at[f, mine], w_s.at[i], w_r.at[i], {"filter": p})
        for i, p in enumerate(peers)
    ]
    blocks = [
        remote(vt, vs.at[pl.ds(1, depth), pl.ds(1 + 2 * f, 2)], v_s.at[i], v_r.at[i], {"filter": p})
        for i, p in enumerate(peers)
    ]
    cots = [
        remote(
            ct.at[:, pl.ds(2 * p, 4)], cg.at[f, pl.ds(1, depth)], c_s.at[i], c_r.at[i], {"filter": p}
        )
        for i, p in enumerate(peers)
    ]
    for group in (weights, cots, blocks):
        for copy in group:
            copy.start()

    vs[:, 0] = jnp.zeros_like(vs[:, 0])
    vs[:, rows + 1] = jnp.zeros_like(vs[:, 0])
    vs[pl.ds(1, depth), pl.ds(1 + 2 * f, 2)] = vt[...]
    cx[pl.ds(1, depth)] = ct[...]
    cg[f, pl.ds(1, depth)] = ct[:, pl.ds(2 * f, 4)]
    wg[f, mine] = wl[mine]

    for copy in halo:
        copy.wait()

    @pl.when(s == 0)
    def _():
        cx[0] = jnp.zeros_like(cx[0])

    @pl.when(s == ns - 1)
    def _():
        cx[depth + 1] = jnp.zeros_like(cx[0])

    edges = []
    for i, p in enumerate(peers):
        for e, plane in enumerate((0, depth + 1)):
            n = 2 * i + e
            edges.append(
                remote(cx.at[plane, pl.ds(2 * p, 4)], cg.at[f, plane], e_s.at[n], e_r.at[n], {"filter": p})
            )
    for copy in edges:
        copy.start()
    for plane in (0, depth + 1):
        cg[f, plane] = cx[plane, pl.ds(2 * f, 4)]

    for copy in weights:
        copy.wait()
    along = []
    for r in range(1, nz):
        target = {"spatial": lax.rem(z + r, nz) * 2 + core}
        along.append(remote(wg.at[:, mine], wg.at[:, mine], x_s.at[r - 1], x_r.at[r - 1], target))
    for copy in along:
        copy.start()
    for copy in blocks:
        copy.wait()
    inner = pl.ds(1, rows)
    planes = [
        remote(vs.at[1, inner], vs.at[depth + 1, inner], q_s.at[0], q_r.at[0], prev),
        remote(vs.at[depth, inner], vs.at[0, inner], q_s.at[1], q_r.at[1], after),
    ]
    for copy in planes:
        copy.start()
    for copy in along:
        copy.wait()
    across = []
    for k in range(nz):
        piece = pl.ds((2 * k + core) * part, part)
        across.append(
            remote(wg.at[:, piece], wg.at[:, piece], y_s.at[k], y_r.at[k], {"spatial": s + 1 - 2 * core})
        )
    for copy in across:
        copy.start()
    for copy in planes:
        copy.wait()

    @pl.when(s == 0)
    def _():
        vs[0] = jnp.zeros_like(vs[0])

    @pl.when(s == ns - 1)
    def _():
        vs[depth + 1] = jnp.zeros_like(vs[0])

    for group in (cots, edges, across):
        for copy in group:
            copy.wait()


def shifted(cells):
    wide = cells.astype(F32)
    lane = lax.broadcasted_iota(jnp.int32, wide.shape, 1)
    below = jnp.where(lane == 0, 0.0, pltpu.roll(wide, 1, 1)).astype(BF)
    above = jnp.where(lane == 127, 0.0, pltpu.roll(wide, 127, 1)).astype(BF)
    return below, cells, above


def spread(src, dst, flip):
    count, channels, _ = src.shape

    def body(i, carry):
        below, here, above = shifted(src[i])
        first, last = (above, below) if flip else (below, above)
        dst[i, pl.ds(0, channels)] = first
        dst[i, pl.ds(channels, channels)] = here
        dst[i, pl.ds(2 * channels, channels)] = last
        return carry

    lax.fori_loop(0, count, body, 0)


def columns(ref, wide, rows_at, flip, pad):
    stack = []
    for sx in range(3):
        for sy in range(3):
            ox, oy = (2 - sx, 2 - sy) if flip else (sx, sy)
            stack.append(jnp.concatenate([ref[(x + ox) * wide + (y + oy)] for x, y in rows_at], axis=1))
    if pad:
        stack.append(jnp.zeros((pad, 128 * len(rows_at)), BF))
    return jnp.concatenate(stack, axis=0)


NT = (((1,), (1,)), ((), ()))


def middle(vs, cx, cg, wg, w1, wm, me, g2, bp, v3o, v3, c3, x3, hs, pre, acc, w1t):
    ns, nf, nm, s, f, m = places()
    depth, rows = 4, 2 * nf
    wide = rows + 2
    w1t[...] = w1[...].T
    spread(vs, v3, False)

    hs[...] = jnp.zeros_like(hs)

    def first(i, carry):
        x, y = i // (rows // 4), lax.rem(i, rows // 4) * 4
        value = jnp.dot(
            w1t[...], columns(v3, wide, [(x, y + j) for j in range(4)], False, 0),
            preferred_element_type=F32,
        )
        hidden = (value * jax.nn.sigmoid(value)).astype(BF)
        for j in range(4):
            pre[x * rows + y + j] = value[:, 128 * j : 128 * (j + 1)]
            hs[x * wide + y + 1 + j] = hidden[:, 128 * j : 128 * (j + 1)]
        return carry

    lax.fori_loop(0, depth * rows // 4, first, 0)

    acc[...] = jnp.zeros_like(acc)
    own = [(x, y) for x in range(depth) for y in range(2)]

    def back(k, carry):
        spread(cg.at[k], c3, True)
        for half in range(2):
            lanes = pl.ds(512 * half, 512)
            acc[:, lanes] += jnp.dot(
                wg[k], columns(c3, 4, own[4 * half : 4 * half + 4], True, 32), preferred_element_type=F32
            )
        return carry

    lax.fori_loop(0, nf, back, 0)
    for n, (x, y) in enumerate(own):
        u = pre[x * rows + 2 * f + y]
        sig = jax.nn.sigmoid(u)
        bp[n] = (acc[:, 128 * n : 128 * (n + 1)] * (sig * (1.0 + u * (1.0 - sig)))).astype(BF)
    for x in range(depth + 2):
        for y in range(4):
            v3o[x * 4 + y] = v3[x * wide + 2 * f + y]

    spread(cx, x3, True)
    me[...] = jnp.zeros_like(me)
    g2[...] = jnp.zeros_like(g2)

    def second(i, carry):
        x, y = i // (rows // 4), lax.rem(i, rows // 4) * 4
        at = [(x, y + j) for j in range(4)]
        field = jnp.concatenate(
            [
                jnp.concatenate([hs[x * wide + y + j + sy] for j in range(4)], axis=1)
                for sy in range(3)
            ],
            axis=0,
        )
        value = jnp.dot(wm[...], field, preferred_element_type=F32)
        lane = lax.broadcasted_iota(jnp.int32, (32, 128), 1)
        for sx in range(3):
            for j in range(4):
                lanes = slice(128 * j, 128 * (j + 1))
                base = 96 * sx
                below = pltpu.roll(value[base : base + 32, lanes], 1, 1)
                above = pltpu.roll(value[base + 64 : base + 96, lanes], 127, 1)
                me[(x + 2 - sx) * rows + y + j] += (
                    jnp.where(lane == 0, 0.0, below)
                    + value[base + 32 : base + 64, lanes]
                    + jnp.where(lane == 127, 0.0, above)
                )
        here = jnp.concatenate([hs[x * wide + y + j + 1] for j in range(4)], axis=1)
        g2[...] += lax.dot_general(here, columns(x3, wide, at, True, 32), NT, preferred_element_type=F32)
        return carry

    lax.fori_loop(0, depth * rows // 4, second, 0)


def final(bh, v3o, bp, w1v, vg, g1, b3):
    spread(bh, b3, True)
    own = [(x, y) for x in range(4) for y in range(2)]
    for half in range(2):
        lanes = pl.ds(512 * half, 512)
        vg[:, lanes] = jnp.dot(
            w1v[...], columns(b3, 4, own[4 * half : 4 * half + 4], True, 0), preferred_element_type=F32
        )
    grads = jnp.concatenate([bp[n] for n in range(8)], axis=1)
    for sx in range(3):
        for sy in range(3):
            field = jnp.concatenate([v3o[(x + sx) * 4 + y + sy] for x, y in own], axis=1)
            k = (sx * 3 + sy) * 192
            g1[k : k + 192] = lax.dot_general(field, grads, NT, preferred_element_type=F32)


def exchange_edges(bp, me, bh, mo, mr, b_s, b_r, m_s, m_r):
    ns, nf, nm, s, f, m = places()
    depth, rows = 4, 2 * nf
    down, up = lax.rem(s + ns - 1, ns), lax.rem(s + 1, ns)
    left, right = lax.rem(f + nf - 1, nf), lax.rem(f + 1, nf)
    targets = [
        {"filter": left}, {"filter": right}, {"spatial": down}, {"spatial": up},
        {"spatial": down, "filter": left}, {"spatial": down, "filter": right},
        {"spatial": up, "filter": left}, {"spatial": up, "filter": right},
    ]
    greet(targets)
    body = pl.ds(0, depth)
    inner = pl.ds(1, depth)
    two, pair = pl.ds(0, 2), pl.ds(1, 2)
    pieces = [
        (bp.at[body, 0], bh.at[inner, 3]),
        (bp.at[body, 1], bh.at[inner, 0]),
        (bp.at[0, two], bh.at[depth + 1, pair]),
        (bp.at[depth - 1, two], bh.at[0, pair]),
        (bp.at[0, 0], bh.at[depth + 1, 3]),
        (bp.at[0, 1], bh.at[depth + 1, 0]),
        (bp.at[depth - 1, 0], bh.at[0, 3]),
        (bp.at[depth - 1, 1], bh.at[0, 0]),
    ]
    copies = [
        remote(src, dst, b_s.at[i], b_r.at[i], target)
        for i, ((src, dst), target) in enumerate(zip(pieces, targets))
    ]
    copies += [
        remote(me.at[pl.ds(0, rows)], mr.at[1], m_s.at[0], m_r.at[0], {"spatial": down}),
        remote(me.at[pl.ds((depth + 1) * rows, rows)], mr.at[0], m_s.at[1], m_r.at[1], {"spatial": up}),
    ]
    for copy in copies:
        copy.start()
    bh[inner, pair] = bp[...]
    mo[...] = me[pl.ds(rows, depth * rows)]
    for copy in copies:
        copy.wait()

    @pl.when(s == 0)
    def _():
        bh[0] = jnp.zeros_like(bh[0])

    @pl.when(s == ns - 1)
    def _():
        bh[depth + 1] = jnp.zeros_like(bh[0])

    @pl.when(f == 0)
    def _():
        bh[:, 0] = jnp.zeros_like(bh[:, 0])

    @pl.when(f == nf - 1)
    def _():
        bh[:, 3] = jnp.zeros_like(bh[:, 0])

    @pl.when(s > 0)
    def _():
        mo[pl.ds(0, rows)] += mr[0]

    @pl.when(s < ns - 1)
    def _():
        mo[pl.ds((depth - 1) * rows, rows)] += mr[1]


def reduce_grads(split, g, out, ra, half, rb, total, rc, a_s, a_r, b_s, b_r, c_s, c_r, d_s, d_r, e_s, e_r):
    ns, nf, nm, s, f, m = places()
    nz = ns // 2
    core, z = lax.rem(s, 2), s // 2
    count = nz * nm
    partner = {"spatial": s + 1 - 2 * core}
    me = z * nm + m

    def peer(r):
        j = lax.rem(me + r, count)
        return j, {"spatial": (j // nm) * 2 + core, "sample": lax.rem(j, nm)}

    greet([partner] + [peer(r)[1] for r in range(1, count)] + [{"filter": lax.rem(f + r, nf)} for r in range(1, nf)])
    a = remote(g.at[1 - core], ra, a_s.at[0], a_r.at[0], partner)
    a.start()
    a.wait()
    half[...] = g[core] + ra[...]
    stage = []
    for r in range(1, count):
        j, target = peer(r)
        stage.append(remote(half.at[j], rb.at[r - 1], b_s.at[r - 1], b_r.at[r - 1], target))
    for copy in stage:
        copy.start()
    value = half[me]
    for r, copy in enumerate(stage):
        copy.wait()
        value = value + rb[r]
    total[...] = value
    first = pl.ds(0, split)
    rc[f] = total[first]
    stage = [
        remote(total.at[first], rc.at[f], c_s.at[r - 1], c_r.at[r - 1], {"filter": lax.rem(f + r, nf)})
        for r in range(1, nf)
    ]
    for copy in stage:
        copy.start()
    for copy in stage:
        copy.wait()
    value = rc[0]
    for k in range(1, nf):
        value = value + rc[k]
    out[core, me, first] = value.astype(BF)
    rest = pl.ds(split, total.shape[0] - split)
    out[core, me, rest] = total[rest].astype(BF)
    stage = []
    for r in range(1, count):
        j, target = peer(r)
        stage.append(remote(out.at[core, me], out.at[core, me], d_s.at[r - 1], d_r.at[r - 1], target))
    for copy in stage:
        copy.start()
    for copy in stage:
        copy.wait()
    e = remote(out.at[core], out.at[core], e_s.at[0], e_r.at[0], partner)
    e.start()
    e.wait()


def on_device(volume, weight_first, weight_second, cotangent):
    ns, nf, nm = lax.axis_size("spatial"), lax.axis_size("filter"), lax.axis_size("sample")
    depth, rows = 4, 2 * nf
    wide = rows + 2
    scaling = 1.0 / math.sqrt(nm * depth * ns * rows * 128)
    nz = ns // 2

    vt = volume[0].transpose(1, 2, 0, 3)
    ct = jnp.pad(cotangent[0].transpose(1, 2, 0, 3), ((0, 0), (1, 1), (0, 0), (0, 0)))
    wl = jnp.pad(weight_second.transpose(1, 0, 2).reshape(128, 864), ((0, 0), (0, 32)))
    wm = weight_second.reshape(3, 3, 3, 128, 32).transpose(0, 2, 4, 1, 3).reshape(288, 384)
    w1 = weight_first.reshape(1728, 128)
    w1v = weight_first.transpose(1, 0, 2).reshape(64, 3456)

    vs, cx, cg, wg = call(
        exchange_inputs,
        3,
        [
            ((depth + 2, wide, 64, 128), BF),
            ((depth + 2, wide, 32, 128), BF),
            ((nf, depth + 2, 4, 32, 128), BF),
            ((nf, 128, 896), BF),
        ],
        [
            dma(nf - 1), dma(nf - 1), dma(nf - 1), dma(nf - 1), dma(2), dma(2),
            dma(2 * nf - 2), dma(2 * nf - 2), dma(nf - 1), dma(nf - 1),
            dma(nz - 1), dma(nz - 1), dma(nz), dma(nz), dma(2), dma(2),
        ],
        0,
    )(vt, ct, wl)

    me, g2, bp, v3o = call(
        middle,
        6,
        [
            (((depth + 2) * rows, 32, 128), F32),
            ((128, 896), F32),
            ((8, 128, 128), BF),
            ((24, 192, 128), BF),
        ],
        [
            pltpu.VMEM(((depth + 2) * wide, 192, 128), BF),
            pltpu.VMEM((24, 96, 128), BF),
            pltpu.VMEM(((depth + 2) * wide, 96, 128), BF),
            pltpu.VMEM((depth * wide, 128, 128), BF),
            pltpu.VMEM((depth * rows, 128, 128), F32),
            pltpu.VMEM((128, 1024), F32),
            pltpu.VMEM((128, 1728), BF),
        ],
    )(
        vs.reshape(-1, 64, 128), cx.reshape(-1, 32, 128), cg.reshape(nf, 24, 32, 128), wg, w1, wm
    )

    bh, mo = call(
        exchange_edges,
        2,
        [((depth + 2, 4, 128, 128), BF), ((depth * rows, 32, 128), F32)],
        [pltpu.VMEM((2, rows, 32, 128), F32), dma(8), dma(8), dma(2), dma(2)],
        1,
    )(bp.reshape(depth, 2, 128, 128), me)

    vg, g1 = call(
        final,
        4,
        [((64, 1024), F32), ((1728, 128), F32)],
        [pltpu.VMEM((24, 384, 128), BF)],
    )(bh.reshape(24, 128, 128), v3o, bp, w1v)

    groups = 2 * nz * nm
    len1 = -(-1728 // (16 * groups)) * 16
    len2 = -(-1024 // (16 * groups)) * 16
    p1 = jnp.pad(g1, ((0, len1 * groups - 1728), (0, 0))).reshape(groups, len1, 128)
    p2 = g2.reshape(128, 7, 128).transpose(1, 0, 2).reshape(896, 128)
    p2 = jnp.pad(p2, ((0, len2 * groups - 896), (0, 0))).reshape(groups, len2, 128)
    length = len1 + len2
    parts = jnp.concatenate([p1, p2], axis=1).reshape(2, nz * nm, length, 128)
    (sums,) = call(
        functools.partial(reduce_grads, len1),
        1,
        [((2, nz * nm, length, 128), BF)],
        [
            pltpu.VMEM((nz * nm, length, 128), F32),
            pltpu.VMEM((nz * nm, length, 128), F32),
            pltpu.VMEM((nz * nm - 1, length, 128), F32),
            pltpu.VMEM((length, 128), F32),
            pltpu.VMEM((nf, len1, 128), F32),
            dma(1), dma(1), dma(nz * nm - 1), dma(nz * nm - 1), dma(nf - 1), dma(nf - 1),
            dma(nz * nm - 1), dma(nz * nm - 1), dma(1), dma(1),
        ],
        2,
    )(parts)
    sums = sums.reshape(groups, length, 128).astype(F32) * scaling
    first_grad = sums[:, :len1].reshape(-1, 128)[:1728].reshape(27, 64, 128)
    s2 = sums[:, len1:].reshape(-1, 128)[:896].reshape(7, 128, 128).transpose(1, 0, 2).reshape(128, 896)
    second_grad = s2[:, :864].reshape(128, 27, 32).transpose(1, 0, 2)
    mapped = mo.reshape(depth, rows, 32, 128).transpose(2, 0, 1, 3)[None]
    volume_grad = vg.reshape(1, 64, depth, 2, 128)
    return (mapped, second_grad, first_grad, volume_grad)


def solution(mesh):
    placed = (
        P("sample", None, "spatial", "filter", None),
        P(),
        P(None, None, "filter"),
        P("sample", "filter", "spatial", None, None),
    )
    return jax.shard_map(
        on_device,
        mesh=mesh,
        in_specs=placed,
        out_specs=(
            P("sample", "filter", "spatial", None, None),
            P(None, None, "filter"),
            P(),
            P("sample", None, "spatial", "filter", None),
        ),
        check_vma=False,
    )
```

time: 797 us -> 175 us (0.22)
  waiting for transfers between devices: 471 us -> 0 us
  matrix products: 252 us -> 0 us
  Pallas kernels: 0 us -> 160 us
  starting transfers between devices: 33.4 us -> 0 us
  between operations: 15.8 us -> 0.75 us
    psum x2 -> x0, waiting for transfers between devices: 268 us -> none  [the longest x1 144 us: on_device(): lax.psum(first_local, ('spatial', 'filter', 'sample')) * scaling]
    dot_general x162 -> x0, matrix products: 252 us -> none  [the longest x54 119 us: backward_terms(): jnp.einsum('io,soxyz->sixyz', weight[offset], piece, preferred_element_ty...]
    unnamed x5 -> x0, waiting for transfers between devices: 163 us -> none
    pallas_call x0 -> x5, Pallas kernels: none -> 160 us  [the longest x1 55.8 us: on_device(): call(middle, 6, [(((depth + 2) * rows, 32, 128), F32), ((128, 896), F32),...]
    ppermute x12 -> x0, starting transfers between devices: 33.1 us -> none  [the longest x6 22.8 us: extended_2(): lax.ppermute(tail, axis, [(i, (i + 1) % count) for i in range(ends)])]
    all_gather x1 -> x0, waiting for transfers between devices: 27.6 us -> none  [on_device(): whole = lax.all_gather(hidden, 'filter', axis=3, tiled=True)]
    ppermute x12 -> x0, waiting for transfers between devices: 11.8 us -> none  [the longest x6 11.3 us: extended_2(): lax.ppermute(head, axis, [((i + 1) % count, i) for i in range(ends)])]
  transfers between devices with their start and end apart: 16 -> 0, of which waited for: 6 -> 0; matrix products, arithmetic and copies ran while one was open for 17% -> 0% of each run, Pallas kernels for 0% -> 0%
where the time goes in v1:
time: 175 us
  Pallas kernels  160 us (91%)
  local copies, waits for them, and re-layouts  11.8 us (7%)
  other arithmetic  2.44 us (1%)
    pallas_call x1, Pallas kernels, on_device(): call(middle, 6, [(((depth + 2) * rows, 32, 128), F32), ((128, 896), F32),...  55.8 us
    pallas_call x1, Pallas kernels, on_device(): call(exchange_inputs, 3, [((depth + 2, wide, 64, 128), BF), ((depth + 2,...  44.5 us
    pallas_call x1, Pallas kernels, on_device(): call(functools.partial(reduce_grads, len1), 1, [((2, nz * nm, length, 128...  35.8 us
    pallas_call x1, Pallas kernels, on_device(): call(exchange_edges, 2, [((depth + 2, 4, 128, 128), BF), ((depth * rows,...  16.9 us
    pallas_call x1, Pallas kernels, on_device(): call(final, 4, [((64, 1024), F32), ((1728, 128), F32)], [pltpu.VMEM((24,...  7.03 us

profile of v1, /device:TPU:1, one launch (start us, length us, event | category | flops | bytes accessed | tf_op | source)
XLA Modules:
  0.0 175.0 jit_solution(9434167524278587852)
XLA Ops:
  0.6 0.0 copy-start.2
  0.6 0.0 copy-start.5
  0.7 1.4 copy.41
  2.1 0.9 pad.16.ct
  3.0 0.0 copy-done.2
  3.0 0.2 copy.26
  3.1 0.7 pad.17.wl
  3.8 0.0 copy-done.5
  3.8 0.7 copy.43
  4.5 44.5 %shard_map.75 = (bf16[6,18,64,128]{3,2,1,0:T(8,128)(2,1)}, bf16[6,18,32,128]{3,2,1,0:T(8,128)(2,1)}, bf16[8,6,4,32,128]{4,3,2,1,0:T(8,128)(2,1)}, bf16[8,128,896]{2,1,0:T(8,128)(2,1)}) custom-call(bf16[4,2,64,128]{3,2,1,0:T(8,128)(2,1)} %bitcast.77, bf16[4,18,32,128]{3,2,1,0:T(8,128)(2,1)} %pad.16.ct, bf16[128,896]{1,0:T(8,128)(2,1)} %pad.17.wl), custom_call_target="tpu_custom_call" | custom-call | tf_op jit(solution)/shard_map/pallas_call | solution.py:432
  49.0 0.2 copy.27
  49.2 0.7 copy.42
  49.9 55.8 %shard_map.76 = (f32[96,32,128]{2,1,0:T(8,128)}, f32[128,896]{1,0:T(8,128)}, bf16[8,128,128]{2,1,0:T(8,128)(2,1)}, bf16[24,192,128]{2,1,0:T(8,128)(2,1)}) custom-call(bf16[108,64,128]{2,1,0:T(8,128)(2,1)} %bitcast.65, bf16[108,32,128]{2,1,0:T(8,128)(2,1)} %bitcast.72, bf16[8,24,32,128]{3,2,1,0:T(8,128)(2,1)} %bitcast.66, ...), custom_call_target="tpu_custom_call" | custom-call | tf_op jit(solution)/shard_map/pallas_call | solution.py:449
  105.7 16.9 %shard_map.77 = (bf16[6,4,128,128]{3,2,1,0:T(8,128)(2,1)}, f32[64,32,128]{2,1,0:T(8,128)}) custom-call(bf16[4,2,128,128]{3,2,1,0:T(8,128)(2,1)} %bitcast.70, f32[96,32,128]{2,1,0:T(8,128)} %get-tuple-element.21.me), custom_call_target="tpu_custom_call" | custom-call | tf_op jit(solution)/shard_map/pallas_call | solution.py:471
  122.6 0.0 copy-done
  122.6 0.8 copy_bitcast_fusion.2.w1v
  123.4 7.0 %shard_map.78 = (f32[64,1024]{1,0:T(8,128)}, f32[1728,128]{1,0:T(8,128)}) custom-call(bf16[24,128,128]{2,1,0:T(8,128)(2,1)} %bitcast.76, bf16[24,192,128]{2,1,0:T(8,128)(2,1)} %get-tuple-element.24.v3o, bf16[8,128,128]{2,1,0:T(8,128)(2,1)} %get-tuple-element.20.bp, bf16[64,3456]{1,0:T(8,128)(2,1)} %copy_bitcast_fusion.2.w1v), custom_call_target="tpu_custom_call" | custom-call | tf_op jit(solution)/shard_map/pallas_call | solution.py:479
  130.5 1.3 pad.18
  131.7 0.0 copy-done.3
  131.8 0.2 copy.30
  132.0 0.2 copy.31
  132.2 1.2 pad_maximum_fusion.g
  133.4 35.8 %shard_map.79 = bf16[2,8,176,128]{3,2,1,0:T(8,128)(2,1)} custom-call(f32[2,8,176,128]{3,2,1,0:T(8,128)} %pad_maximum_fusion.g), custom_call_target="tpu_custom_call" | custom-call | tf_op jit(solution)/shard_map/pallas_call | solution.py:494
  169.2 1.2 convert_multiply_fusion
  170.4 0.1 slice.21
  170.5 1.0 slice.22
  171.5 0.2 copy.32
  171.7 0.8 slice.20
  172.5 0.0 copy-done.4
  172.5 0.9 reshape.97
  173.4 0.0 copy-done.1
  173.4 1.6 copy.40
  (6 shorter events, 0.1 us)
Async XLA Ops:
  0.6 2.3 %copy-start.2 = (bf16[27,128,32]{1,2,0:T(8,128)(2,1)S(1)}, bf16[27,128,32]{1,2,0:T(8,128)(2,1)}, u32[]{:S(2)}) copy-start(bf16[27,128,32]{1,2,0:T(8,128)(2,1)} %param.6) | copy-start | bytes 663556
  0.6 3.2 %copy-start.5 = (bf16[1,64,4,2,128]{4,3,2,1,0:T(2,128)(2,1)S(1)}, bf16[1,64,4,2,128]{4,3,2,1,0:T(2,128)(2,1)}, u32[]{:S(2)}) copy-start(bf16[1,64,4,2,128]{4,3,2,1,0:T(2,128)(2,1)} %param.4) | copy-start | bytes 393220
  105.7 16.9 %copy-start = (bf16[27,64,128]{2,1,0:T(8,128)(2,1)S(1)}, bf16[27,64,128]{2,1,0:T(8,128)(2,1)}, u32[]{:S(2)}) copy-start(bf16[27,64,128]{2,1,0:T(8,128)(2,1)} %param.5) | copy-start | bytes 1327108
  130.5 1.3 copy-start.3
  171.5 1.0 copy-start.4
  171.5 2.0 %copy-start.1 = (f32[64,32,128]{2,1,0:T(8,128)S(1)}, f32[64,32,128]{2,1,0:T(8,128)}, u32[]{:S(2)}) copy-start(f32[64,32,128]{2,1,0:T(8,128)} %get-tuple-element.22) | copy-start | bytes 3145732

commit v2 on v1

--- a/solution.py
+++ b/solution.py
@@ -174,16 +174,18 @@
 
 def spread(src, dst, flip):
     count, channels, _ = src.shape
+    step = 6 if count % 6 == 0 else 4
 
     def body(i, carry):
-        below, here, above = shifted(src[i])
-        first, last = (above, below) if flip else (below, above)
-        dst[i, pl.ds(0, channels)] = first
-        dst[i, pl.ds(channels, channels)] = here
-        dst[i, pl.ds(2 * channels, channels)] = last
+        for u in range(step):
+            below, here, above = shifted(src[i * step + u])
+            first, last = (above, below) if flip else (below, above)
+            dst[i * step + u, pl.ds(0, channels)] = first
+            dst[i * step + u, pl.ds(channels, channels)] = here
+            dst[i * step + u, pl.ds(2 * channels, channels)] = last
         return carry
 
-    lax.fori_loop(0, count, body, 0)
+    lax.fori_loop(0, count // step, body, 0)
 
 
 def columns(ref, wide, rows_at, flip, pad):
@@ -209,19 +211,21 @@
 
     hs[...] = jnp.zeros_like(hs)
 
+    group = min(8, rows)
+
     def first(i, carry):
-        x, y = i // (rows // 4), lax.rem(i, rows // 4) * 4
+        x, y = i // (rows // group), lax.rem(i, rows // group) * group
         value = jnp.dot(
-            w1t[...], columns(v3, wide, [(x, y + j) for j in range(4)], False, 0),
+            w1t[...], columns(v3, wide, [(x, y + j) for j in range(group)], False, 0),
             preferred_element_type=F32,
         )
         hidden = (value * jax.nn.sigmoid(value)).astype(BF)
-        for j in range(4):
+        for j in range(group):
             pre[x * rows + y + j] = value[:, 128 * j : 128 * (j + 1)]
             hs[x * wide + y + 1 + j] = hidden[:, 128 * j : 128 * (j + 1)]
         return carry
 
-    lax.fori_loop(0, depth * rows // 4, first, 0)
+    lax.fori_loop(0, depth * rows // group, first, 0)
 
     acc[...] = jnp.zeros_like(acc)
     own = [(x, y) for x in range(depth) for y in range(2)]

time: 175 us -> 148 us (0.85)
  Pallas kernels: 160 us -> 133 us
    pallas_call x1, Pallas kernels: 55.8 us -> 29.8 us  [on_device(): call(middle, 6, [(((depth + 2) * rows, 32, 128), F32), ((128, 896), F32),...]
where the time goes in v2:
time: 148 us
  Pallas kernels  133 us (90%)
  local copies, waits for them, and re-layouts  11.8 us (8%)
  other arithmetic  2.44 us (2%)
    pallas_call x1, Pallas kernels, on_device(): call(exchange_inputs, 3, [((depth + 2, wide, 64, 128), BF), ((depth + 2,...  44.5 us
    pallas_call x1, Pallas kernels, on_device(): call(functools.partial(reduce_grads, len1), 1, [((2, nz * nm, length, 128...  35.8 us
    pallas_call x1, Pallas kernels, on_device(): call(middle, 6, [(((depth + 2) * rows, 32, 128), F32), ((128, 896), F32),...  29.8 us
    pallas_call x1, Pallas kernels, on_device(): call(exchange_edges, 2, [((depth + 2, 4, 128, 128), BF), ((depth * rows,...  16.8 us
    pallas_call x1, Pallas kernels, on_device(): call(final, 4, [((64, 1024), F32), ((1728, 128), F32)], [pltpu.VMEM((24,...  5.6 us

profile of v2, /device:TPU:1, one launch (start us, length us, event | category | flops | bytes accessed | tf_op | source)
XLA Modules:
  0.0 147.6 jit_solution(17773627303201675765)
XLA Ops:
  0.6 0.0 copy-start.2
  0.6 0.0 copy-start.5
  0.7 1.4 copy.41
  2.1 0.9 pad.16.ct
  3.0 0.0 copy-done.2
  3.0 0.2 copy.26
  3.1 0.7 pad.17.wl
  3.8 0.0 copy-done.5
  3.8 0.7 copy.43
  4.5 44.5 %shard_map.75 = (bf16[6,18,64,128]{3,2,1,0:T(8,128)(2,1)}, bf16[6,18,32,128]{3,2,1,0:T(8,128)(2,1)}, bf16[8,6,4,32,128]{4,3,2,1,0:T(8,128)(2,1)}, bf16[8,128,896]{2,1,0:T(8,128)(2,1)}) custom-call(bf16[4,2,64,128]{3,2,1,0:T(8,128)(2,1)} %bitcast.77, bf16[4,18,32,128]{3,2,1,0:T(8,128)(2,1)} %pad.16.ct, bf16[128,896]{1,0:T(8,128)(2,1)} %pad.17.wl), custom_call_target="tpu_custom_call" | custom-call | tf_op jit(solution)/shard_map/pallas_call | solution.py:436
  49.0 0.2 copy.27
  49.2 0.7 copy.42
  49.9 29.8 %shard_map.76 = (f32[96,32,128]{2,1,0:T(8,128)}, f32[128,896]{1,0:T(8,128)}, bf16[8,128,128]{2,1,0:T(8,128)(2,1)}, bf16[24,192,128]{2,1,0:T(8,128)(2,1)}) custom-call(bf16[108,64,128]{2,1,0:T(8,128)(2,1)} %bitcast.65, bf16[108,32,128]{2,1,0:T(8,128)(2,1)} %bitcast.72, bf16[8,24,32,128]{3,2,1,0:T(8,128)(2,1)} %bitcast.66, ...), custom_call_target="tpu_custom_call" | custom-call | tf_op jit(solution)/shard_map/pallas_call | solution.py:453
  79.8 16.8 %shard_map.77 = (bf16[6,4,128,128]{3,2,1,0:T(8,128)(2,1)}, f32[64,32,128]{2,1,0:T(8,128)}) custom-call(bf16[4,2,128,128]{3,2,1,0:T(8,128)(2,1)} %bitcast.70, f32[96,32,128]{2,1,0:T(8,128)} %get-tuple-element.21.me), custom_call_target="tpu_custom_call" | custom-call | tf_op jit(solution)/shard_map/pallas_call | solution.py:475
  96.6 0.0 copy-done
  96.6 0.8 copy_bitcast_fusion.2.w1v
  97.4 5.6 %shard_map.78 = (f32[64,1024]{1,0:T(8,128)}, f32[1728,128]{1,0:T(8,128)}) custom-call(bf16[24,128,128]{2,1,0:T(8,128)(2,1)} %bitcast.76, bf16[24,192,128]{2,1,0:T(8,128)(2,1)} %get-tuple-element.24.v3o, bf16[8,128,128]{2,1,0:T(8,128)(2,1)} %get-tuple-element.20.bp, bf16[64,3456]{1,0:T(8,128)(2,1)} %copy_bitcast_fusion.2.w1v), custom_call_target="tpu_custom_call" | custom-call | tf_op jit(solution)/shard_map/pallas_call | solution.py:483
  103.0 1.3 pad.18
  104.3 0.0 copy-done.3
  104.3 0.2 copy.30
  104.5 0.2 copy.31
  104.8 1.2 pad_maximum_fusion.g
  106.0 35.8 %shard_map.79 = bf16[2,8,176,128]{3,2,1,0:T(8,128)(2,1)} custom-call(f32[2,8,176,128]{3,2,1,0:T(8,128)} %pad_maximum_fusion.g), custom_call_target="tpu_custom_call" | custom-call | tf_op jit(solution)/shard_map/pallas_call | solution.py:498
  141.8 1.2 convert_multiply_fusion
  143.0 0.1 slice.21
  143.0 1.0 slice.22
  144.1 0.2 copy.32
  144.3 0.8 slice.20
  145.1 0.0 copy-done.4
  145.1 0.9 reshape.97
  146.0 0.0 copy-done.1
  146.0 1.6 %copy.40 = f32[4,16,32,128]{3,1,0,2:T(8,128)} copy(f32[4,16,32,128]{3,2,1,0:T(8,128)S(1)} %bitcast.68) | data formatting | bytes 2097152 | tf_op jit(solution)/shard_map/reshape | solution.py:517
  (6 shorter events, 0.1 us)
Async XLA Ops:
  0.6 2.3 %copy-start.2 = (bf16[27,128,32]{1,2,0:T(8,128)(2,1)S(1)}, bf16[27,128,32]{1,2,0:T(8,128)(2,1)}, u32[]{:S(2)}) copy-start(bf16[27,128,32]{1,2,0:T(8,128)(2,1)} %param.6) | copy-start | bytes 663556
  0.6 3.2 %copy-start.5 = (bf16[1,64,4,2,128]{4,3,2,1,0:T(2,128)(2,1)S(1)}, bf16[1,64,4,2,128]{4,3,2,1,0:T(2,128)(2,1)}, u32[]{:S(2)}) copy-start(bf16[1,64,4,2,128]{4,3,2,1,0:T(2,128)(2,1)} %param.4) | copy-start | bytes 393220
  79.7 16.9 %copy-start = (bf16[27,64,128]{2,1,0:T(8,128)(2,1)S(1)}, bf16[27,64,128]{2,1,0:T(8,128)(2,1)}, u32[]{:S(2)}) copy-start(bf16[27,64,128]{2,1,0:T(8,128)(2,1)} %param.5) | copy-start | bytes 1327108
  103.0 1.3 copy-start.3
  144.0 1.0 copy-start.4
  144.0 2.0 %copy-start.1 = (f32[64,32,128]{2,1,0:T(8,128)S(1)}, f32[64,32,128]{2,1,0:T(8,128)}, u32[]{:S(2)}) copy-start(f32[64,32,128]{2,1,0:T(8,128)} %get-tuple-element.22) | copy-start | bytes 3145732

commit v3 on v0

v3 whole, which is shorter than its diff:
```python
import functools
import math

import jax
import jax.numpy as jnp
from jax import lax
from jax.experimental import pallas as pl
from jax.experimental.pallas import tpu as pltpu
from jax.sharding import PartitionSpec as P

MESH = pl.DeviceIdType.MESH
BF = jnp.bfloat16
F32 = jnp.float32
VMEM = pl.BlockSpec(memory_space=pltpu.VMEM)
LIMIT = 56 * 1024 * 1024


def remote(src, dst, send, recv, device):
    return pltpu.make_async_remote_copy(
        src_ref=src, dst_ref=dst, send_sem=send, recv_sem=recv, device_id=device, device_id_type=MESH
    )


def greet(partners):
    barrier = pltpu.get_barrier_semaphore()
    for partner in partners:
        pl.semaphore_signal(barrier, inc=1, device_id=partner, device_id_type=MESH)
    pl.semaphore_wait(barrier, len(partners))


def places():
    ns, nf, nm = lax.axis_size("spatial"), lax.axis_size("filter"), lax.axis_size("sample")
    s, f, m = lax.axis_index("spatial"), lax.axis_index("filter"), lax.axis_index("sample")
    return ns, nf, nm, s, f, m


def dma(n):
    return pltpu.SemaphoreType.DMA((n,))


def shifted(cells):
    wide = cells.astype(F32)
    lane = lax.broadcasted_iota(jnp.int32, wide.shape, 1)
    below = jnp.where(lane == 0, 0.0, pltpu.roll(wide, 1, 1)).astype(BF)
    above = jnp.where(lane == 127, 0.0, pltpu.roll(wide, 127, 1)).astype(BF)
    return below, cells, above


def spread(src, dst, flip):
    count, channels, _ = src.shape
    step = 6 if count % 6 == 0 else 4

    def body(i, carry):
        for u in range(step):
            below, here, above = shifted(src[i * step + u])
            first, last = (above, below) if flip else (below, above)
            dst[i * step + u, pl.ds(0, channels)] = first
            dst[i * step + u, pl.ds(channels, channels)] = here
            dst[i * step + u, pl.ds(2 * channels, channels)] = last
        return carry

    lax.fori_loop(0, count // step, body, 0)


def columns(ref, wide, rows_at, flip, pad):
    stack = []
    for sx in range(3):
        for sy in range(3):
            ox, oy = (2 - sx, 2 - sy) if flip else (sx, sy)
            stack.append(jnp.concatenate([ref[(x + ox) * wide + (y + oy)] for x, y in rows_at], axis=1))
    if pad:
        stack.append(jnp.zeros((pad, 128 * len(rows_at)), BF))
    return jnp.concatenate(stack, axis=0)


NT = (((1,), (1,)), ((), ()))


class Links:
    def __init__(self, send, recv):
        self.send, self.recv, self.used = send, recv, 0

    def __call__(self, src, dst, device):
        n = self.used
        self.used += 1
        return remote(src, dst, self.send.at[n], self.recv.at[n], device)


def start(copies):
    for copy in copies:
        copy.start()


def wait(copies):
    for copy in copies:
        copy.wait()


def zero(ref):
    ref[...] = jnp.zeros(ref.shape, ref.dtype)


class Summed:
    def __init__(self, links, at, rows, whole, from_core, half, from_peers, total, from_filter, held):
        self.links, self.at, self.rows = links, at, rows
        self.whole, self.from_core, self.half, self.from_peers = whole, from_core, half, from_peers
        self.total, self.from_filter, self.held = total, from_filter, held

    def core(self):
        ns, nf, nm, s, f, m = self.at
        span = self.half.shape[0]
        core = lax.rem(s, 2)
        partner = {"spatial": s + 1 - 2 * core}
        self.moving = [self.links(self.whole.at[pl.ds((1 - core) * span, span)], self.from_core, partner)]
        start(self.moving)

    def peers(self):
        ns, nf, nm, s, f, m = self.at
        span, rows = self.half.shape[0], self.rows
        core, count = lax.rem(s, 2), span // rows
        me = (s // 2) * nm + m
        wait(self.moving)
        self.half[...] = self.whole[pl.ds(core * span, span)] + self.from_core[...]
        self.targets = []
        self.moving = []
        for r in range(1, count):
            j = lax.rem(me + r, count)
            device = {"spatial": (j // nm) * 2 + core, "sample": lax.rem(j, nm)}
            self.targets.append(device)
            self.moving.append(self.links(self.half.at[pl.ds(j * rows, rows)], self.from_peers.at[r - 1], device))
        start(self.moving)

    def gather_sum(self):
        ns, nf, nm, s, f, m = self.at
        wait(self.moving)
        value = self.half[pl.ds(((s // 2) * nm + m) * self.rows, self.rows)]
        for r in range(len(self.moving)):
            value = value + self.from_peers[r]
        return value

    def filters(self):
        ns, nf, nm, s, f, m = self.at
        value = self.gather_sum()
        self.total[...] = value
        self.from_filter[f] = value
        self.moving = [
            self.links(self.total, self.from_filter.at[f], {"filter": lax.rem(f + r, nf)}) for r in range(1, nf)
        ]
        start(self.moving)

    def back(self):
        ns, nf, nm, s, f, m = self.at
        if self.from_filter is None:
            value = self.gather_sum()
        else:
            wait(self.moving)
            value = self.from_filter[0]
            for k in range(1, nf):
                value = value + self.from_filter[k]
        span, rows = self.half.shape[0], self.rows
        self.base = pl.ds(lax.rem(s, 2) * span, span)
        mine = pl.ds(lax.rem(s, 2) * span + ((s // 2) * nm + m) * rows, rows)
        self.held[mine] = value.astype(BF)
        self.moving = [self.links(self.held.at[mine], self.held.at[mine], device) for device in self.targets]
        start(self.moving)

    def across(self):
        s = self.at[3]
        wait(self.moving)
        self.moving = [
            self.links(self.held.at[self.base], self.held.at[self.base], {"spatial": s + 1 - 2 * lax.rem(s, 2)})
        ]
        start(self.moving)

    def finish(self):
        wait(self.moving)


DEPTH = 4
OWN = [(x, y) for x in range(DEPTH) for y in range(2)]


def whole_step(
    scaling, vt, ct, wl, w1, mo, g2o, g1o, vg,
    vs, cx, cg, wg, v3, c3, x3, hs, pre, acc, w1t, w1v, wm, me, mr, bp, bh, b3, v3o, g2a,
    g1w, g1c, g1h, g1p, g1t, g1f, g1b, g2w, g2c, g2h, g2p, g2b, send, recv,
):
    at = ns, nf, nm, s, f, m = places()
    links = Links(send, recv)
    depth, rows = DEPTH, 2 * nf
    wide = rows + 2
    part = wl.shape[0] // ns
    nz = ns // 2
    core, z = lax.rem(s, 2), s // 2
    down, up = lax.rem(s + ns - 1, ns), lax.rem(s + 1, ns)
    left, right = lax.rem(f + nf - 1, nf), lax.rem(f + 1, nf)
    prev, after = {"spatial": down}, {"spatial": up}
    peers = [lax.rem(f + r, nf) for r in range(1, nf)]
    edges = [
        {"filter": left}, {"filter": right}, prev, after,
        {"spatial": down, "filter": left}, {"spatial": down, "filter": right},
        {"spatial": up, "filter": left}, {"spatial": up, "filter": right},
    ]
    group = []
    for r in range(1, nz * nm):
        j = lax.rem(z * nm + m + r, nz * nm)
        group.append({"spatial": (j // nm) * 2 + core, "sample": lax.rem(j, nm)})
    greet([{"filter": p} for p in peers] + edges[2:] + group)

    inner, body, two, pair = pl.ds(1, depth), pl.ds(0, depth), pl.ds(0, 2), pl.ds(1, 2)
    block = pl.ds(1 + 2 * f, 2)
    blocks = [links(vt, vs.at[inner, block], {"filter": p}) for p in peers]
    mine = pl.ds(s * part, part)
    halo = [links(ct.at[0], cx.at[depth + 1], prev), links(ct.at[depth - 1], cx.at[0], after)]
    weights = [links(wl.at[mine], wg.at[f, mine], {"filter": p}) for p in peers]
    cots = [links(ct.at[:, pl.ds(2 * p, 4)], cg.at[f, inner], {"filter": p}) for p in peers]
    for copies in (blocks, weights, halo, cots):
        start(copies)

    vs[:, 0] = jnp.zeros_like(vs[:, 0])
    vs[:, rows + 1] = jnp.zeros_like(vs[:, 0])
    vs[inner, block] = vt[...]
    cx[inner] = ct[...]
    cg[f, inner] = ct[:, pl.ds(2 * f, 4)]
    wg[f, mine] = wl[mine]
    w1t[...] = w1[...].T
    wlt = wl[...].T
    for sx in range(3):
        for sy in range(3):
            for sz in range(3):
                k = sx * 9 + sy * 3 + sz
                w1v[:, 128 * k : 128 * (k + 1)] = w1[64 * k : 64 * (k + 1)]
                j = 32 * (sx * 3 + sz)
                wm[j : j + 32, 128 * sy : 128 * (sy + 1)] = wlt[32 * k : 32 * (k + 1)]
    zero(hs)
    zero(me)
    zero(acc)
    zero(g2a)

    wait(halo)

    @pl.when(s == 0)
    def _():
        cx[0] = jnp.zeros_like(cx[0])

    @pl.when(s == ns - 1)
    def _():
        cx[depth + 1] = jnp.zeros_like(cx[0])

    cxr = cx.reshape((depth + 2) * wide, 32, 128)
    spread(cxr, x3, True)
    for plane in (0, depth + 1):
        cg[f, plane] = cx[plane, pl.ds(2 * f, 4)]

    wait(weights)
    along = [
        links(wg.at[:, mine], wg.at[:, mine], {"spatial": lax.rem(z + r, nz) * 2 + core}) for r in range(1, nz)
    ]
    start(along)

    wait(blocks)
    row = pl.ds(1, rows)
    planes = [links(vs.at[1, row], vs.at[depth + 1, row], prev), links(vs.at[depth, row], vs.at[0, row], after)]
    start(planes)
    vsr = vs.reshape((depth + 2) * wide, 64, 128)
    spread(vsr.at[pl.ds(wide, depth * wide)], v3.at[pl.ds(wide, depth * wide)], False)
    lot = min(8, rows)
    times = rows // lot

    def first(i, carry):
        x, y = i // times, lax.rem(i, times) * lot
        value = jnp.dot(
            w1t[...], columns(v3, wide, [(x, y + j) for j in range(lot)], False, 0), preferred_element_type=F32
        )
        hidden = (value * jax.nn.sigmoid(value)).astype(BF)
        for j in range(lot):
            pre[x * rows + y + j] = value[:, 128 * j : 128 * (j + 1)]
            hs[x * wide + y + 1 + j] = hidden[:, 128 * j : 128 * (j + 1)]
        return carry

    lax.fori_loop(times, 3 * times, first, 0)
    wait(along)
    across = []
    for k in range(nz):
        piece = pl.ds((2 * k + core) * part, part)
        across.append(links(wg.at[:, piece], wg.at[:, piece], {"spatial": s + 1 - 2 * core}))
    start(across)
    wait(planes)

    @pl.when(s == 0)
    def _():
        vs[0] = jnp.zeros_like(vs[0])

    @pl.when(s == ns - 1)
    def _():
        vs[depth + 1] = jnp.zeros_like(vs[0])

    for plane in (0, depth + 1):
        span = pl.ds(plane * wide, wide)
        spread(vsr.at[span], v3.at[span], False)
    lax.fori_loop(0, times, first, 0)
    lax.fori_loop(3 * times, 4 * times, first, 0)

    forward = []
    for r, copy in enumerate(cots):
        copy.wait()
        k = lax.rem(f + nf - 1 - r, nf)
        pieces = [links(cg.at[k, 1], cg.at[k, depth + 1], prev), links(cg.at[k, depth], cg.at[k, 0], after)]
        start(pieces)
        forward += pieces

    def second_weights(i, carry):
        x, y = i // times, lax.rem(i, times) * lot
        here = jnp.concatenate([hs[x * wide + y + j + 1] for j in range(lot)], axis=1)
        field = columns(x3, wide, [(x, y + j) for j in range(lot)], True, 32)
        g2a[...] += lax.dot_general(here, field, NT, preferred_element_type=F32)
        return carry

    lax.fori_loop(0, 2 * times, second_weights, 0)
    wait(across)
    wait(forward)

    @pl.when(s == 0)
    def _():
        cg[:, 0] = jnp.zeros_like(cg[:, 0])

    @pl.when(s == ns - 1)
    def _():
        cg[:, depth + 1] = jnp.zeros_like(cg[:, 0])

    cgr = cg.reshape(nf, (depth + 2) * 4, 32, 128)

    def back(k, carry):
        spread(cgr.at[k], c3, True)
        for part_at in range(2):
            lanes = pl.ds(512 * part_at, 512)
            acc[:, lanes] += jnp.dot(
                wg[k], columns(c3, 4, OWN[4 * part_at : 4 * part_at + 4], True, 32), preferred_element_type=F32
            )
        return carry

    lax.fori_loop(0, nf, back, 0)
    for n, (x, y) in enumerate(OWN):
        u = pre[x * rows + 2 * f + y]
        sig = jax.nn.sigmoid(u)
        bp[x, y] = (acc[:, 128 * n : 128 * (n + 1)] * (sig * (1.0 + u * (1.0 - sig)))).astype(BF)
    pieces = [
        (bp.at[body, 0], bh.at[inner, 3]), (bp.at[body, 1], bh.at[inner, 0]),
        (bp.at[0, two], bh.at[depth + 1, pair]), (bp.at[depth - 1, two], bh.at[0, pair]),
        (bp.at[0, 0], bh.at[depth + 1, 3]), (bp.at[0, 1], bh.at[depth + 1, 0]),
        (bp.at[depth - 1, 0], bh.at[0, 3]), (bp.at[depth - 1, 1], bh.at[0, 0]),
    ]
    cells = [links(src, dst, device) for (src, dst), device in zip(pieces, edges)]
    start(cells)
    bh[inner, pair] = bp[...]

    for x in range(depth + 2):
        for y in range(4):
            v3o[x * 4 + y] = v3[x * wide + 2 * f + y]
    grads = jnp.concatenate([bp[x, y] for x, y in OWN], axis=1)
    for j in range(9):
        sx, sy = j // 3, j % 3
        field = jnp.concatenate([v3o[(x + sx) * 4 + y + sy] for x, y in OWN], axis=1)
        g1w[192 * j : 192 * (j + 1)] = lax.dot_general(field, grads, NT, preferred_element_type=F32)
    g1w[1728:] = jnp.zeros((g1w.shape[0] - 1728, 128), F32)
    one = Summed(links, at, g1t.shape[0], g1w, g1c, g1h, g1p, g1t, g1f, g1b)
    one.core()

    lax.fori_loop(2 * times, 3 * times, second_weights, 0)
    one.peers()
    lax.fori_loop(3 * times, 4 * times, second_weights, 0)
    for t in range(7):
        g2w[128 * t : 128 * (t + 1)] = g2a[:, 128 * t : 128 * (t + 1)]
    g2w[896:] = jnp.zeros((g2w.shape[0] - 896, 128), F32)
    other = Summed(links, at, g2p.shape[1], g2w, g2c, g2h, g2p, None, None, g2b)
    other.core()

    def second(i, carry):
        x, y = i // (rows // 4), lax.rem(i, rows // 4) * 4
        field = jnp.concatenate(
            [jnp.concatenate([hs[x * wide + y + j + sy] for j in range(4)], axis=1) for sy in range(3)],
            axis=0,
        )
        value = jnp.dot(wm[...], field, preferred_element_type=F32)
        lane = lax.broadcasted_iota(jnp.int32, (32, 128), 1)
        for sx in range(3):
            for j in range(4):
                lanes = slice(128 * j, 128 * (j + 1))
                base = 96 * sx
                below = pltpu.roll(value[base : base + 32, lanes], 1, 1)
                above = pltpu.roll(value[base + 64 : base + 96, lanes], 127, 1)
                me[(x + 2 - sx) * rows + y + j] += (
                    jnp.where(lane == 0, 0.0, below)
                    + value[base + 32 : base + 64, lanes]
                    + jnp.where(lane == 127, 0.0, above)
                )
        return carry

    turn = rows // 4
    lax.fori_loop(0, turn, second, 0)
    one.filters()
    other.peers()
    lax.fori_loop(turn, 2 * turn, second, 0)
    lax.fori_loop(2 * turn, 3 * turn, second, 0)
    one.back()
    other.back()
    lax.fori_loop(3 * turn, 4 * turn, second, 0)
    outer = [
        links(me.at[pl.ds(0, rows)], mr.at[1], prev),
        links(me.at[pl.ds((depth + 1) * rows, rows)], mr.at[0], after),
    ]
    start(outer)

    wait(cells)

    @pl.when(s == 0)
    def _():
        bh[0] = jnp.zeros_like(bh[0])

    @pl.when(s == ns - 1)
    def _():
        bh[depth + 1] = jnp.zeros_like(bh[0])

    @pl.when(f == 0)
    def _():
        bh[:, 0] = jnp.zeros_like(bh[:, 0])

    @pl.when(f == nf - 1)
    def _():
        bh[:, 3] = jnp.zeros_like(bh[:, 0])

    one.across()
    other.across()
    spread(bh.reshape((depth + 2) * 4, 128, 128), b3, True)
    for part_at in range(2):
        lanes = pl.ds(512 * part_at, 512)
        vg[:, lanes] = jnp.dot(
            w1v[...], columns(b3, 4, OWN[4 * part_at : 4 * part_at + 4], True, 0), preferred_element_type=F32
        )

    mo[...] = me[pl.ds(rows, depth * rows)]
    wait(outer)

    @pl.when(s > 0)
    def _():
        mo[pl.ds(0, rows)] += mr[0]

    @pl.when(s < ns - 1)
    def _():
        mo[pl.ds((depth - 1) * rows, rows)] += mr[1]

    one.finish()
    other.finish()
    g1o[...] = g1b[0:1728].astype(F32) * scaling
    for k in range(27):
        tile = g2b[128 * (k // 4) : 128 * (k // 4 + 1)].astype(F32) * scaling
        g2o[k] = tile[:, 32 * (k % 4) : 32 * (k % 4 + 1)]


def on_device(volume, weight_first, weight_second, cotangent):
    ns, nf, nm = lax.axis_size("spatial"), lax.axis_size("filter"), lax.axis_size("sample")
    depth, rows = DEPTH, 2 * nf
    wide = rows + 2
    scaling = 1.0 / math.sqrt(nm * depth * ns * rows * 128)
    count = ns // 2 * nm

    vt = volume[0].transpose(1, 2, 0, 3)
    ct = jnp.pad(cotangent[0].transpose(1, 2, 0, 3), ((0, 0), (1, 1), (0, 0), (0, 0)))
    wl = jnp.pad(weight_second.transpose(1, 0, 2).reshape(128, 864), ((0, 0), (0, 32)))
    w1 = weight_first.reshape(1728, 128)

    len1 = -(-1728 // (32 * count)) * 16
    len2 = -(-1024 // (32 * count)) * 16
    slab = (depth + 2) * wide
    scratch = [
        ((depth + 2, wide, 64, 128), BF), ((depth + 2, wide, 32, 128), BF),
        ((nf, depth + 2, 4, 32, 128), BF), ((nf, 128, 896), BF),
        ((slab, 192, 128), BF), ((24, 96, 128), BF), ((slab, 96, 128), BF),
        ((depth * wide, 128, 128), BF), ((depth * rows, 128, 128), F32), ((128, 1024), F32),
        ((128, 1728), BF), ((64, 3456), BF), ((288, 384), BF),
        (((depth + 2) * rows, 32, 128), F32), ((2, rows, 32, 128), F32),
        ((depth, 2, 128, 128), BF), ((depth + 2, 4, 128, 128), BF), ((24, 384, 128), BF),
        ((24, 192, 128), BF), ((128, 896), F32),
        ((2 * count * len1, 128), F32), ((count * len1, 128), F32), ((count * len1, 128), F32),
        ((count - 1, len1, 128), F32), ((len1, 128), F32), ((nf, len1, 128), F32),
        ((2 * count * len1, 128), BF),
        ((2 * count * len2, 128), F32), ((count * len2, 128), F32), ((count * len2, 128), F32),
        ((count - 1, len2, 128), F32), ((2 * count * len2, 128), BF),
    ]
    copies = 128
    mo, g2o, g1o, vg = pl.pallas_call(
        functools.partial(whole_step, scaling),
        out_shape=[
            jax.ShapeDtypeStruct((depth * rows, 32, 128), F32),
            jax.ShapeDtypeStruct((27, 128, 32), F32),
            jax.ShapeDtypeStruct((1728, 128), F32),
            jax.ShapeDtypeStruct((64, 1024), F32),
        ],
        in_specs=[VMEM] * 4,
        out_specs=[VMEM] * 4,
        scratch_shapes=[pltpu.VMEM(shape, dtype) for shape, dtype in scratch] + [dma(copies), dma(copies)],
        compiler_params=pltpu.CompilerParams(
            vmem_limit_bytes=LIMIT, collective_id=0, has_side_effects=True
        ),
    )(vt, ct, wl, w1)
    mapped = mo.reshape(depth, rows, 32, 128).transpose(2, 0, 1, 3)[None]
    return (mapped, g2o, g1o.reshape(27, 64, 128), vg.reshape(1, 64, depth, 2, 128))


def solution(mesh):
    placed = (
        P("sample", None, "spatial", "filter", None),
        P(),
        P(None, None, "filter"),
        P("sample", "filter", "spatial", None, None),
    )
    return jax.shard_map(
        on_device,
        mesh=mesh,
        in_specs=placed,
        out_specs=(
            P("sample", "filter", "spatial", None, None),
            P(None, None, "filter"),
            P(),
            P("sample", None, "spatial", "filter", None),
        ),
        check_vma=False,
    )
```

time: 797 us -> 108 us (0.14)
  waiting for transfers between devices: 471 us -> 0 us
  matrix products: 252 us -> 0 us
  Pallas kernels: 0 us -> 95.2 us
  starting transfers between devices: 33.4 us -> 0 us
  between operations: 15.8 us -> 0.66 us
  other arithmetic: 10.4 us -> 0 us
    psum x2 -> x0, waiting for transfers between devices: 268 us -> none  [the longest x1 144 us: on_device(): lax.psum(first_local, ('spatial', 'filter', 'sample')) * scaling]
    dot_general x162 -> x0, matrix products: 252 us -> none  [the longest x54 119 us: backward_terms(): jnp.einsum('io,soxyz->sixyz', weight[offset], piece, preferred_element_ty...]
    unnamed x5 -> x0, waiting for transfers between devices: 163 us -> none
    pallas_call x0 -> x1, Pallas kernels: none -> 95.2 us  [on_device(): pl.pallas_call(functools.partial(whole_step, scaling), out_shape=[jax.Sha...]
    ppermute x12 -> x0, starting transfers between devices: 33.1 us -> none  [the longest x6 22.8 us: extended_2(): lax.ppermute(tail, axis, [(i, (i + 1) % count) for i in range(ends)])]
    all_gather x1 -> x0, waiting for transfers between devices: 27.6 us -> none  [on_device(): whole = lax.all_gather(hidden, 'filter', axis=3, tiled=True)]
    ppermute x12 -> x0, waiting for transfers between devices: 11.8 us -> none  [the longest x6 11.3 us: extended_2(): lax.ppermute(head, axis, [((i + 1) % count, i) for i in range(ends)])]
  transfers between devices with their start and end apart: 16 -> 0, of which waited for: 6 -> 0; matrix products, arithmetic and copies ran while one was open for 17% -> 0% of each run, Pallas kernels for 0% -> 0%
where the time goes in v3:
time: 108 us
  Pallas kernels  95.2 us (88%)
  local copies, waits for them, and re-layouts  11.7 us (11%)
    pallas_call x1, Pallas kernels, on_device(): pl.pallas_call(functools.partial(whole_step, scaling), out_shape=[jax.Sha...  95.2 us
    unnamed x10, local copies, waits for them, and re-layouts  5.16 us
    reshape x1, local copies, waits for them, and re-layouts, on_device(): mapped = mo.reshape(depth, rows, 32, 128).transpose(2, 0, 1, 3)[None]  2.95 us

profile of v3, /device:TPU:1, one launch (start us, length us, event | category | flops | bytes accessed | tf_op | source)
XLA Modules:
  0.0 107.6 jit_solution(1395892525353970003)
XLA Ops:
  0.6 1.6 %copy.23 = bf16[1,64,4,2,128]{4,1,3,2,0:T(8,128)(2,1)} copy(bf16[1,64,4,2,128]{4,3,2,1,0:T(2,128)(2,1)} %param.4) | data formatting | bytes 262144 | tf_op args[0]
  2.2 1.1 %copy.15 = bf16[128,864]{1,0:T(8,128)(2,1)S(1)} copy(bf16[128,864]{0,1:T(8,128)(2,1)} %bitcast.27) | data formatting | bytes 442368 | tf_op jit(solution)/shard_map/reshape | solution.py:469
  3.3 0.7 pad.9.wl
  4.0 1.4 %copy.22 = bf16[1,32,4,16,128]{4,1,3,2,0:T(8,128)(2,1)S(1)} copy(bf16[1,32,4,16,128]{4,3,2,1,0:T(8,128)(2,1)} %param.7) | data formatting | bytes 1048576 | tf_op args[3]
  5.4 0.9 pad.8.ct
  6.3 95.2 %shard_map.75 = (f32[64,32,128]{2,1,0:T(8,128)}, f32[27,128,32]{2,1,0:T(8,128)}, f32[1728,128]{1,0:T(8,128)}, f32[64,1024]{1,0:T(8,128)}) custom-call(bf16[4,2,64,128]{3,2,1,0:T(8,128)(2,1)} %bitcast.25, bf16[4,18,32,128]{3,2,1,0:T(8,128)(2,1)} %pad.8.ct, bf16[128,896]{1,0:T(8,128)(2,1)} %pad.9.wl, bf16[1728,128]{1,0:T(8,128)(2,1)} %bitcast.26), custom_call_target="tpu_custom_call" | custom-call | tf_op jit(solution)/shard_map/pallas_call | solution.py:491
  101.5 0.0 copy-start.2
  101.5 0.0 copy-start
  101.5 2.9 %copy.21 = f32[4,16,32,128]{3,1,0,2:T(8,128)} copy(f32[4,16,32,128]{3,2,1,0:T(8,128)} %bitcast.23) | data formatting | bytes 2097152 | tf_op jit(solution)/shard_map/reshape | solution.py:506
  104.4 0.0 copy-start.1
  104.4 0.0 copy-done.2
  104.4 0.9 reshape.27
  105.4 0.0 copy-done
  105.4 1.3 %copy.17 = f32[27,128,32]{1,2,0:T(8,128)} copy(f32[27,128,32]{2,1,0:T(8,128)S(1)} %copy-done) | data formatting | bytes 884736
  106.6 0.0 copy-done.1
  106.6 0.9 copy.25
Async XLA Ops:
  101.5 3.0 %copy-start.2 = (f32[64,1024]{1,0:T(8,128)S(1)}, f32[64,1024]{1,0:T(8,128)}, u32[]{:S(2)}) copy-start(f32[64,1024]{1,0:T(8,128)} %get-tuple-element.11) | copy-start | bytes 786436
  101.5 3.9 %copy-start = (f32[27,128,32]{2,1,0:T(8,128)S(1)}, f32[27,128,32]{2,1,0:T(8,128)}, u32[]{:S(2)}) copy-start(f32[27,128,32]{2,1,0:T(8,128)} %get-tuple-element.17) | copy-start | bytes 1327108
  104.4 2.2 %copy-start.1 = (f32[1728,128]{1,0:T(8,128)S(1)}, f32[1728,128]{1,0:T(8,128)}, u32[]{:S(2)}) copy-start(f32[1728,128]{1,0:T(8,128)} %get-tuple-element.10) | copy-start | bytes 2654212

commit v4 on v3

--- a/solution.py
+++ b/solution.py
@@ -214,7 +214,7 @@
     halo = [links(ct.at[0], cx.at[depth + 1], prev), links(ct.at[depth - 1], cx.at[0], after)]
     weights = [links(wl.at[mine], wg.at[f, mine], {"filter": p}) for p in peers]
     cots = [links(ct.at[:, pl.ds(2 * p, 4)], cg.at[f, inner], {"filter": p}) for p in peers]
-    for copies in (blocks, weights, halo, cots):
+    for copies in (weights, halo, blocks):
         start(copies)
 
     vs[:, 0] = jnp.zeros_like(vs[:, 0])
@@ -262,6 +262,7 @@
     row = pl.ds(1, rows)
     planes = [links(vs.at[1, row], vs.at[depth + 1, row], prev), links(vs.at[depth, row], vs.at[0, row], after)]
     start(planes)
+    start(cots)
     vsr = vs.reshape((depth + 2) * wide, 64, 128)
     spread(vsr.at[pl.ds(wide, depth * wide)], v3.at[pl.ds(wide, depth * wide)], False)
     lot = min(8, rows)
@@ -301,6 +302,15 @@
     lax.fori_loop(0, times, first, 0)
     lax.fori_loop(3 * times, 4 * times, first, 0)
 
+    def second_weights(i, carry):
+        x, y = i // times, lax.rem(i, times) * lot
+        here = jnp.concatenate([hs[x * wide + y + j + 1] for j in range(lot)], axis=1)
+        field = columns(x3, wide, [(x, y + j) for j in range(lot)], True, 32)
+        g2a[...] += lax.dot_general(here, field, NT, preferred_element_type=F32)
+        return carry
+
+    lax.fori_loop(0, 3 * times, second_weights, 0)
+
     forward = []
     for r, copy in enumerate(cots):
         copy.wait()
@@ -309,14 +319,19 @@
         start(pieces)
         forward += pieces
 
-    def second_weights(i, carry):
-        x, y = i // times, lax.rem(i, times) * lot
-        here = jnp.concatenate([hs[x * wide + y + j + 1] for j in range(lot)], axis=1)
-        field = columns(x3, wide, [(x, y + j) for j in range(lot)], True, 32)
-        g2a[...] += lax.dot_general(here, field, NT, preferred_element_type=F32)
+    cgr = cg.reshape(nf, (depth + 2) * 4, 32, 128)
+
+    def inside(k, carry):
+        spread(cgr.at[k, pl.ds(4, 4 * depth)], c3.at[k, pl.ds(4, 4 * depth)], True)
         return carry
 
-    lax.fori_loop(0, 2 * times, second_weights, 0)
+    lax.fori_loop(0, nf, inside, 0)
+    lax.fori_loop(3 * times, 4 * times, second_weights, 0)
+    for t in range(7):
+        g2w[128 * t : 128 * (t + 1)] = g2a[:, 128 * t : 128 * (t + 1)]
+    g2w[896:] = jnp.zeros((g2w.shape[0] - 896, 128), F32)
+    other = Summed(links, at, g2p.shape[1], g2w, g2c, g2h, g2p, None, None, g2b)
+    other.core()
     wait(across)
     wait(forward)
 
@@ -328,14 +343,14 @@
     def _():
         cg[:, depth + 1] = jnp.zeros_like(cg[:, 0])
 
-    cgr = cg.reshape(nf, (depth + 2) * 4, 32, 128)
-
     def back(k, carry):
-        spread(cgr.at[k], c3, True)
+        for plane in (0, depth + 1):
+            span = pl.ds(4 * plane, 4)
+            spread(cgr.at[k, span], c3.at[k, span], True)
         for part_at in range(2):
             lanes = pl.ds(512 * part_at, 512)
             acc[:, lanes] += jnp.dot(
-                wg[k], columns(c3, 4, OWN[4 * part_at : 4 * part_at + 4], True, 32), preferred_element_type=F32
+                wg[k], columns(c3.at[k], 4, OWN[4 * part_at : 4 * part_at + 4], True, 32), preferred_element_type=F32
             )
         return carry
 
@@ -366,14 +381,7 @@
     one = Summed(links, at, g1t.shape[0], g1w, g1c, g1h, g1p, g1t, g1f, g1b)
     one.core()
 
-    lax.fori_loop(2 * times, 3 * times, second_weights, 0)
-    one.peers()
-    lax.fori_loop(3 * times, 4 * times, second_weights, 0)
-    for t in range(7):
-        g2w[128 * t : 128 * (t + 1)] = g2a[:, 128 * t : 128 * (t + 1)]
-    g2w[896:] = jnp.zeros((g2w.shape[0] - 896, 128), F32)
-    other = Summed(links, at, g2p.shape[1], g2w, g2c, g2h, g2p, None, None, g2b)
-    other.core()
+    other.peers()
 
     def second(i, carry):
         x, y = i // (rows // 4), lax.rem(i, rows // 4) * 4
@@ -397,19 +405,16 @@
         return carry
 
     turn = rows // 4
-    lax.fori_loop(0, turn, second, 0)
-    one.filters()
-    other.peers()
-    lax.fori_loop(turn, 2 * turn, second, 0)
-    lax.fori_loop(2 * turn, 3 * turn, second, 0)
-    one.back()
-    other.back()
-    lax.fori_loop(3 * turn, 4 * turn, second, 0)
+    lax.fori_loop(0, 2 * turn, second, 0)
+    one.peers()
+    lax.fori_loop(2 * turn, 4 * turn, second, 0)
     outer = [
         links(me.at[pl.ds(0, rows)], mr.at[1], prev),
         links(me.at[pl.ds((depth + 1) * rows, rows)], mr.at[0], after),
     ]
     start(outer)
+    one.filters()
+    other.back()
 
     wait(cells)
 
@@ -429,8 +434,6 @@
     def _():
         bh[:, 3] = jnp.zeros_like(bh[:, 0])
 
-    one.across()
-    other.across()
     spread(bh.reshape((depth + 2) * 4, 128, 128), b3, True)
     for part_at in range(2):
         lanes = pl.ds(512 * part_at, 512)
@@ -438,6 +441,8 @@
             w1v[...], columns(b3, 4, OWN[4 * part_at : 4 * part_at + 4], True, 0), preferred_element_type=F32
         )
 
+    one.back()
+    other.across()
     mo[...] = me[pl.ds(rows, depth * rows)]
     wait(outer)
 
@@ -449,6 +454,7 @@
     def _():
         mo[pl.ds((depth - 1) * rows, rows)] += mr[1]
 
+    one.across()
     one.finish()
     other.finish()
     g1o[...] = g1b[0:1728].astype(F32) * scaling
@@ -475,7 +481,7 @@
     scratch = [
         ((depth + 2, wide, 64, 128), BF), ((depth + 2, wide, 32, 128), BF),
         ((nf, depth + 2, 4, 32, 128), BF), ((nf, 128, 896), BF),
-        ((slab, 192, 128), BF), ((24, 96, 128), BF), ((slab, 96, 128), BF),
+        ((slab, 192, 128), BF), ((nf, 24, 96, 128), BF), ((slab, 96, 128), BF),
         ((depth * wide, 128, 128), BF), ((depth * rows, 128, 128), F32), ((128, 1024), F32),
         ((128, 1728), BF), ((64, 3456), BF), ((288, 384), BF),
         (((depth + 2) * rows, 32, 128), F32), ((2, rows, 32, 128), F32),

time: 108 us -> 99.6 us (0.922)
  Pallas kernels: 95.2 us -> 87 us
    pallas_call x1, Pallas kernels: 95.2 us -> 87 us  [on_device(): pl.pallas_call(functools.partial(whole_step, scaling), out_shape=[jax.Sha...]
where the time goes in v4:
time: 99.6 us; the launch traced here: 99.3 us
  Pallas kernels  87 us (87%)
  local copies, waits for them, and re-layouts  11.7 us (12%)
    pallas_call x1, Pallas kernels, on_device(): pl.pallas_call(functools.partial(whole_step, scaling), out_shape=[jax.Sha...  87 us
    unnamed x10, local copies, waits for them, and re-layouts  5.16 us
    reshape x1, local copies, waits for them, and re-layouts, on_device(): mapped = mo.reshape(depth, rows, 32, 128).transpose(2, 0, 1, 3)[None]  2.95 us

profile of v4, /device:TPU:1, one launch (start us, length us, event | category | flops | bytes accessed | tf_op | source)
XLA Modules:
  0.0 99.3 jit_solution(6775697695390745606)
XLA Ops:
  0.6 1.6 %copy.23 = bf16[1,64,4,2,128]{4,1,3,2,0:T(8,128)(2,1)} copy(bf16[1,64,4,2,128]{4,3,2,1,0:T(2,128)(2,1)} %param.4) | data formatting | bytes 262144 | tf_op args[0]
  2.2 1.1 %copy.15 = bf16[128,864]{1,0:T(8,128)(2,1)S(1)} copy(bf16[128,864]{0,1:T(8,128)(2,1)} %bitcast.27) | data formatting | bytes 442368 | tf_op jit(solution)/shard_map/reshape | solution.py:475
  3.3 0.7 pad.9.wl
  4.0 1.4 %copy.22 = bf16[1,32,4,16,128]{4,1,3,2,0:T(8,128)(2,1)S(1)} copy(bf16[1,32,4,16,128]{4,3,2,1,0:T(8,128)(2,1)} %param.7) | data formatting | bytes 1048576 | tf_op args[3]
  5.4 0.9 pad.8.ct
  6.3 87.0 %shard_map.75 = (f32[64,32,128]{2,1,0:T(8,128)}, f32[27,128,32]{2,1,0:T(8,128)}, f32[1728,128]{1,0:T(8,128)}, f32[64,1024]{1,0:T(8,128)}) custom-call(bf16[4,2,64,128]{3,2,1,0:T(8,128)(2,1)} %bitcast.25, bf16[4,18,32,128]{3,2,1,0:T(8,128)(2,1)} %pad.8.ct, bf16[128,896]{1,0:T(8,128)(2,1)} %pad.9.wl, bf16[1728,128]{1,0:T(8,128)(2,1)} %bitcast.26), custom_call_target="tpu_custom_call" | custom-call | tf_op jit(solution)/shard_map/pallas_call | solution.py:497
  93.3 0.0 copy-start.2
  93.3 0.0 copy-start
  93.3 2.9 %copy.21 = f32[4,16,32,128]{3,1,0,2:T(8,128)} copy(f32[4,16,32,128]{3,2,1,0:T(8,128)} %bitcast.23) | data formatting | bytes 2097152 | tf_op jit(solution)/shard_map/reshape | solution.py:512
  96.2 0.0 copy-start.1
  96.2 0.0 copy-done.2
  96.2 0.9 reshape.27
  97.1 0.0 copy-done
  97.1 1.3 %copy.17 = f32[27,128,32]{1,2,0:T(8,128)} copy(f32[27,128,32]{2,1,0:T(8,128)S(1)} %copy-done) | data formatting | bytes 884736
  98.4 0.0 copy-done.1
  98.4 0.9 copy.25
Async XLA Ops:
  93.3 3.0 %copy-start.2 = (f32[64,1024]{1,0:T(8,128)S(1)}, f32[64,1024]{1,0:T(8,128)}, u32[]{:S(2)}) copy-start(f32[64,1024]{1,0:T(8,128)} %get-tuple-element.11) | copy-start | bytes 786436
  93.3 3.9 %copy-start = (f32[27,128,32]{2,1,0:T(8,128)S(1)}, f32[27,128,32]{2,1,0:T(8,128)}, u32[]{:S(2)}) copy-start(f32[27,128,32]{2,1,0:T(8,128)} %get-tuple-element.17) | copy-start | bytes 1327108
  96.2 2.2 %copy-start.1 = (f32[1728,128]{1,0:T(8,128)S(1)}, f32[1728,128]{1,0:T(8,128)}, u32[]{:S(2)}) copy-start(f32[1728,128]{1,0:T(8,128)} %get-tuple-element.10) | copy-start | bytes 2654212

commit v5 on v4

--- a/solution.py
+++ b/solution.py
@@ -177,12 +177,37 @@
 
 
 DEPTH = 4
+
+
+def around(block, padded):
+    body, inner, two, pair = pl.ds(0, DEPTH), pl.ds(1, DEPTH), pl.ds(0, 2), pl.ds(1, 2)
+    last = DEPTH - 1
+    return [
+        (block.at[body, 0], padded.at[inner, 3]), (block.at[body, 1], padded.at[inner, 0]),
+        (block.at[0, two], padded.at[DEPTH + 1, pair]), (block.at[last, two], padded.at[0, pair]),
+        (block.at[0, 0], padded.at[DEPTH + 1, 3]), (block.at[0, 1], padded.at[DEPTH + 1, 0]),
+        (block.at[last, 0], padded.at[0, 3]), (block.at[last, 1], padded.at[0, 0]),
+    ]
+
+
+def clear_outside(padded, at):
+    ns, nf, nm, s, f, m = at
+    for place, end, plane in ((s, 0, 0), (s, ns - 1, DEPTH + 1)):
+        @pl.when(place == end)
+        def _():
+            padded[plane] = jnp.zeros_like(padded[plane])
+    for place, end, row in ((f, 0, 0), (f, nf - 1, 3)):
+        @pl.when(place == end)
+        def _():
+            padded[:, row] = jnp.zeros_like(padded[:, row])
+
+
 OWN = [(x, y) for x in range(DEPTH) for y in range(2)]
 
 
 def whole_step(
     scaling, vt, ct, wl, w1, mo, g2o, g1o, vg,
-    vs, cx, cg, wg, v3, c3, x3, hs, pre, acc, w1t, w1v, wm, me, mr, bp, bh, b3, v3o, g2a,
+    vs, vo, cx, cg, wg, v3, c3, x3, hs, pre, acc, w1t, w1v, wm, me, mr, bp, bh, b3, v3o, g2a,
     g1w, g1c, g1h, g1p, g1t, g1f, g1b, g2w, g2c, g2h, g2p, g2b, send, recv,
 ):
     at = ns, nf, nm, s, f, m = places()
@@ -214,7 +239,8 @@
     halo = [links(ct.at[0], cx.at[depth + 1], prev), links(ct.at[depth - 1], cx.at[0], after)]
     weights = [links(wl.at[mine], wg.at[f, mine], {"filter": p}) for p in peers]
     cots = [links(ct.at[:, pl.ds(2 * p, 4)], cg.at[f, inner], {"filter": p}) for p in peers]
-    for copies in (weights, halo, blocks):
+    corners = [links(src, dst, device) for (src, dst), device in zip(around(vt, vo), edges)]
+    for copies in (weights, halo, corners, cots):
         start(copies)
 
     vs[:, 0] = jnp.zeros_like(vs[:, 0])
@@ -237,79 +263,36 @@
     zero(acc)
     zero(g2a)
 
-    wait(halo)
-
-    @pl.when(s == 0)
-    def _():
-        cx[0] = jnp.zeros_like(cx[0])
-
-    @pl.when(s == ns - 1)
-    def _():
-        cx[depth + 1] = jnp.zeros_like(cx[0])
-
-    cxr = cx.reshape((depth + 2) * wide, 32, 128)
-    spread(cxr, x3, True)
-    for plane in (0, depth + 1):
-        cg[f, plane] = cx[plane, pl.ds(2 * f, 4)]
-
     wait(weights)
     along = [
         links(wg.at[:, mine], wg.at[:, mine], {"spatial": lax.rem(z + r, nz) * 2 + core}) for r in range(1, nz)
     ]
     start(along)
 
-    wait(blocks)
-    row = pl.ds(1, rows)
-    planes = [links(vs.at[1, row], vs.at[depth + 1, row], prev), links(vs.at[depth, row], vs.at[0, row], after)]
-    start(planes)
-    start(cots)
-    vsr = vs.reshape((depth + 2) * wide, 64, 128)
-    spread(vsr.at[pl.ds(wide, depth * wide)], v3.at[pl.ds(wide, depth * wide)], False)
-    lot = min(8, rows)
-    times = rows // lot
-
-    def first(i, carry):
-        x, y = i // times, lax.rem(i, times) * lot
-        value = jnp.dot(
-            w1t[...], columns(v3, wide, [(x, y + j) for j in range(lot)], False, 0), preferred_element_type=F32
+    wait(halo)
+
+    @pl.when(s == 0)
+    def _():
+        cx[0] = jnp.zeros_like(cx[0])
+
+    @pl.when(s == ns - 1)
+    def _():
+        cx[depth + 1] = jnp.zeros_like(cx[0])
+
+    cxr = cx.reshape((depth + 2) * wide, 32, 128)
+    spread(cxr, x3, True)
+    for plane in (0, depth + 1):
+        cg[f, plane] = cx[plane, pl.ds(2 * f, 4)]
+
+    wait(corners)
+    vo[inner, pair] = vt[...]
+    clear_outside(vo, at)
+    spread(vo.reshape((depth + 2) * 4, 64, 128), v3o, False)
+    for part_at in range(2):
+        lanes = pl.ds(512 * part_at, 512)
+        pre[:, lanes] = jnp.dot(
+            w1t[...], columns(v3o, 4, OWN[4 * part_at : 4 * part_at + 4], False, 0), preferred_element_type=F32
         )
-        hidden = (value * jax.nn.sigmoid(value)).astype(BF)
-        for j in range(lot):
-            pre[x * rows + y + j] = value[:, 128 * j : 128 * (j + 1)]
-            hs[x * wide + y + 1 + j] = hidden[:, 128 * j : 128 * (j + 1)]
-        return carry
-
-    lax.fori_loop(times, 3 * times, first, 0)
-    wait(along)
-    across = []
-    for k in range(nz):
-        piece = pl.ds((2 * k + core) * part, part)
-        across.append(links(wg.at[:, piece], wg.at[:, piece], {"spatial": s + 1 - 2 * core}))
-    start(across)
-    wait(planes)
-
-    @pl.when(s == 0)
-    def _():
-        vs[0] = jnp.zeros_like(vs[0])
-
-    @pl.when(s == ns - 1)
-    def _():
-        vs[depth + 1] = jnp.zeros_like(vs[0])
-
-    for plane in (0, depth + 1):
-        span = pl.ds(plane * wide, wide)
-        spread(vsr.at[span], v3.at[span], False)
-    lax.fori_loop(0, times, first, 0)
-    lax.fori_loop(3 * times, 4 * times, first, 0)
-
-    def second_weights(i, carry):
-        x, y = i // times, lax.rem(i, times) * lot
-        here = jnp.concatenate([hs[x * wide + y + j + 1] for j in range(lot)], axis=1)
-        field = columns(x3, wide, [(x, y + j) for j in range(lot)], True, 32)
-        g2a[...] += lax.dot_general(here, field, NT, preferred_element_type=F32)
-        return carry
-
-    lax.fori_loop(0, 3 * times, second_weights, 0)
 
     forward = []
     for r, copy in enumerate(cots):
@@ -319,6 +302,7 @@
         start(pieces)
         forward += pieces
 
+    start(blocks)
     cgr = cg.reshape(nf, (depth + 2) * 4, 32, 128)
 
     def inside(k, carry):
@@ -326,12 +310,12 @@
         return carry
 
     lax.fori_loop(0, nf, inside, 0)
-    lax.fori_loop(3 * times, 4 * times, second_weights, 0)
-    for t in range(7):
-        g2w[128 * t : 128 * (t + 1)] = g2a[:, 128 * t : 128 * (t + 1)]
-    g2w[896:] = jnp.zeros((g2w.shape[0] - 896, 128), F32)
-    other = Summed(links, at, g2p.shape[1], g2w, g2c, g2h, g2p, None, None, g2b)
-    other.core()
+    wait(along)
+    across = []
+    for k in range(nz):
+        piece = pl.ds((2 * k + core) * part, part)
+        across.append(links(wg.at[:, piece], wg.at[:, piece], {"spatial": s + 1 - 2 * core}))
+    start(across)
     wait(across)
     wait(forward)
 
@@ -356,22 +340,13 @@
 
     lax.fori_loop(0, nf, back, 0)
     for n, (x, y) in enumerate(OWN):
-        u = pre[x * rows + 2 * f + y]
+        u = pre[:, 128 * n : 128 * (n + 1)]
         sig = jax.nn.sigmoid(u)
         bp[x, y] = (acc[:, 128 * n : 128 * (n + 1)] * (sig * (1.0 + u * (1.0 - sig)))).astype(BF)
-    pieces = [
-        (bp.at[body, 0], bh.at[inner, 3]), (bp.at[body, 1], bh.at[inner, 0]),
-        (bp.at[0, two], bh.at[depth + 1, pair]), (bp.at[depth - 1, two], bh.at[0, pair]),
-        (bp.at[0, 0], bh.at[depth + 1, 3]), (bp.at[0, 1], bh.at[depth + 1, 0]),
-        (bp.at[depth - 1, 0], bh.at[0, 3]), (bp.at[depth - 1, 1], bh.at[0, 0]),
-    ]
-    cells = [links(src, dst, device) for (src, dst), device in zip(pieces, edges)]
+    cells = [links(src, dst, device) for (src, dst), device in zip(around(bp, bh), edges)]
     start(cells)
     bh[inner, pair] = bp[...]
 
-    for x in range(depth + 2):
-        for y in range(4):
-            v3o[x * 4 + y] = v3[x * wide + 2 * f + y]
     grads = jnp.concatenate([bp[x, y] for x, y in OWN], axis=1)
     for j in range(9):
         sx, sy = j // 3, j % 3
@@ -381,7 +356,58 @@
     one = Summed(links, at, g1t.shape[0], g1w, g1c, g1h, g1p, g1t, g1f, g1b)
     one.core()
 
-    other.peers()
+    wait(blocks)
+    row = pl.ds(1, rows)
+    planes = [links(vs.at[1, row], vs.at[depth + 1, row], prev), links(vs.at[depth, row], vs.at[0, row], after)]
+    start(planes)
+    vsr = vs.reshape((depth + 2) * wide, 64, 128)
+    spread(vsr.at[pl.ds(wide, depth * wide)], v3.at[pl.ds(wide, depth * wide)], False)
+    lot = min(8, rows)
+    times = rows // lot
+
+    def first(i, carry):
+        x, y = i // times, lax.rem(i, times) * lot
+        value = jnp.dot(
+            w1t[...], columns(v3, wide, [(x, y + j) for j in range(lot)], False, 0), preferred_element_type=F32
+        )
+        hidden = (value * jax.nn.sigmoid(value)).astype(BF)
+        for j in range(lot):
+            hs[x * wide + y + 1 + j] = hidden[:, 128 * j : 128 * (j + 1)]
+        return carry
+
+    lax.fori_loop(times, 3 * times, first, 0)
+    one.peers()
+    wait(planes)
+
+    @pl.when(s == 0)
+    def _():
+        vs[0] = jnp.zeros_like(vs[0])
+
+    @pl.when(s == ns - 1)
+    def _():
+        vs[depth + 1] = jnp.zeros_like(vs[0])
+
+    for plane in (0, depth + 1):
+        span = pl.ds(plane * wide, wide)
+        spread(vsr.at[span], v3.at[span], False)
+    lax.fori_loop(0, times, first, 0)
+    lax.fori_loop(3 * times, 4 * times, first, 0)
+    one.filters()
+
+    def second_weights(i, carry):
+        x, y = i // times, lax.rem(i, times) * lot
+        here = jnp.concatenate([hs[x * wide + y + j + 1] for j in range(lot)], axis=1)
+        field = columns(x3, wide, [(x, y + j) for j in range(lot)], True, 32)
+        g2a[...] += lax.dot_general(here, field, NT, preferred_element_type=F32)
+        return carry
+
+    lax.fori_loop(0, 4 * times, second_weights, 0)
+    for t in range(7):
+        g2w[128 * t : 128 * (t + 1)] = g2a[:, 128 * t : 128 * (t + 1)]
+    g2w[896:] = jnp.zeros((g2w.shape[0] - 896, 128), F32)
+    other = Summed(links, at, g2p.shape[1], g2w, g2c, g2h, g2p, None, None, g2b)
+    other.core()
+    one.back()
 
     def second(i, carry):
         x, y = i // (rows // 4), lax.rem(i, rows // 4) * 4
@@ -406,43 +432,27 @@
 
     turn = rows // 4
     lax.fori_loop(0, 2 * turn, second, 0)
-    one.peers()
+    other.peers()
+    one.across()
     lax.fori_loop(2 * turn, 4 * turn, second, 0)
     outer = [
         links(me.at[pl.ds(0, rows)], mr.at[1], prev),
         links(me.at[pl.ds((depth + 1) * rows, rows)], mr.at[0], after),
     ]
     start(outer)
-    one.filters()
     other.back()
 
     wait(cells)
-
-    @pl.when(s == 0)
-    def _():
-        bh[0] = jnp.zeros_like(bh[0])
-
-    @pl.when(s == ns - 1)
-    def _():
-        bh[depth + 1] = jnp.zeros_like(bh[0])
-
-    @pl.when(f == 0)
-    def _():
-        bh[:, 0] = jnp.zeros_like(bh[:, 0])
-
-    @pl.when(f == nf - 1)
-    def _():
-        bh[:, 3] = jnp.zeros_like(bh[:, 0])
-
+    clear_outside(bh, at)
     spread(bh.reshape((depth + 2) * 4, 128, 128), b3, True)
     for part_at in range(2):
         lanes = pl.ds(512 * part_at, 512)
         vg[:, lanes] = jnp.dot(
             w1v[...], columns(b3, 4, OWN[4 * part_at : 4 * part_at + 4], True, 0), preferred_element_type=F32
         )
-
-    one.back()
     other.across()
+    one.finish()
+    g1o[...] = g1b[0:1728].astype(F32) * scaling
     mo[...] = me[pl.ds(rows, depth * rows)]
     wait(outer)
 
@@ -454,10 +464,7 @@
     def _():
         mo[pl.ds((depth - 1) * rows, rows)] += mr[1]
 
-    one.across()
-    one.finish()
     other.finish()
-    g1o[...] = g1b[0:1728].astype(F32) * scaling
     for k in range(27):
         tile = g2b[128 * (k // 4) : 128 * (k // 4 + 1)].astype(F32) * scaling
         g2o[k] = tile[:, 32 * (k % 4) : 32 * (k % 4 + 1)]
@@ -479,10 +486,10 @@
     len2 = -(-1024 // (32 * count)) * 16
     slab = (depth + 2) * wide
     scratch = [
-        ((depth + 2, wide, 64, 128), BF), ((depth + 2, wide, 32, 128), BF),
+        ((depth + 2, wide, 64, 128), BF), ((depth + 2, 4, 64, 128), BF), ((depth + 2, wide, 32, 128), BF),
         ((nf, depth + 2, 4, 32, 128), BF), ((nf, 128, 896), BF),
         ((slab, 192, 128), BF), ((nf, 24, 96, 128), BF), ((slab, 96, 128), BF),
-        ((depth * wide, 128, 128), BF), ((depth * rows, 128, 128), F32), ((128, 1024), F32),
+        ((depth * wide, 128, 128), BF), ((128, 1024), F32), ((128, 1024), F32),
         ((128, 1728), BF), ((64, 3456), BF), ((288, 384), BF),
         (((depth + 2) * rows, 32, 128), F32), ((2, rows, 32, 128), F32),
         ((depth, 2, 128, 128), BF), ((depth + 2, 4, 128, 128), BF), ((24, 384, 128), BF),

time: 99.6 us -> 97.4 us (0.978)
  Pallas kernels: 87 us -> 84.8 us
    pallas_call x1, Pallas kernels: 87 us -> 84.8 us  [on_device(): pl.pallas_call(functools.partial(whole_step, scaling), out_shape=[jax.Sha...]
where the time goes in v5:
time: 97.4 us; the launch traced here: 97.2 us
  Pallas kernels  84.8 us (87%)
  local copies, waits for them, and re-layouts  11.7 us (12%)
    pallas_call x1, Pallas kernels, on_device(): pl.pallas_call(functools.partial(whole_step, scaling), out_shape=[jax.Sha...  84.8 us
    unnamed x10, local copies, waits for them, and re-layouts  5.16 us
    reshape x1, local copies, waits for them, and re-layouts, on_device(): mapped = mo.reshape(depth, rows, 32, 128).transpose(2, 0, 1, 3)[None]  2.95 us

profile of v5, /device:TPU:1, one launch (start us, length us, event | category | flops | bytes accessed | tf_op | source)
XLA Modules:
  0.0 97.2 jit_solution(363857060887949284)
XLA Ops:
  0.6 1.6 %copy.23 = bf16[1,64,4,2,128]{4,1,3,2,0:T(8,128)(2,1)} copy(bf16[1,64,4,2,128]{4,3,2,1,0:T(2,128)(2,1)} %param.4) | data formatting | bytes 262144 | tf_op args[0]
  2.2 1.1 %copy.15 = bf16[128,864]{1,0:T(8,128)(2,1)S(1)} copy(bf16[128,864]{0,1:T(8,128)(2,1)} %bitcast.27) | data formatting | bytes 442368 | tf_op jit(solution)/shard_map/reshape | solution.py:482
  3.3 0.7 pad.9.wl
  4.0 1.4 %copy.22 = bf16[1,32,4,16,128]{4,1,3,2,0:T(8,128)(2,1)S(1)} copy(bf16[1,32,4,16,128]{4,3,2,1,0:T(8,128)(2,1)} %param.7) | data formatting | bytes 1048576 | tf_op args[3]
  5.4 0.9 pad.8.ct
  6.3 84.8 %shard_map.75 = (f32[64,32,128]{2,1,0:T(8,128)}, f32[27,128,32]{2,1,0:T(8,128)}, f32[1728,128]{1,0:T(8,128)}, f32[64,1024]{1,0:T(8,128)}) custom-call(bf16[4,2,64,128]{3,2,1,0:T(8,128)(2,1)} %bitcast.25, bf16[4,18,32,128]{3,2,1,0:T(8,128)(2,1)} %pad.8.ct, bf16[128,896]{1,0:T(8,128)(2,1)} %pad.9.wl, bf16[1728,128]{1,0:T(8,128)(2,1)} %bitcast.26), custom_call_target="tpu_custom_call" | custom-call | tf_op jit(solution)/shard_map/pallas_call | solution.py:504
  91.1 0.0 copy-start.2
  91.1 0.0 copy-start
  91.1 2.9 %copy.21 = f32[4,16,32,128]{3,1,0,2:T(8,128)} copy(f32[4,16,32,128]{3,2,1,0:T(8,128)} %bitcast.23) | data formatting | bytes 2097152 | tf_op jit(solution)/shard_map/reshape | solution.py:519
  94.1 0.0 copy-start.1
  94.1 0.0 copy-done.2
  94.1 0.9 reshape.27
  95.0 0.0 copy-done
  95.0 1.3 %copy.17 = f32[27,128,32]{1,2,0:T(8,128)} copy(f32[27,128,32]{2,1,0:T(8,128)S(1)} %copy-done) | data formatting | bytes 884736
  96.3 0.0 copy-done.1
  96.3 0.9 copy.25
Async XLA Ops:
  91.1 3.0 %copy-start.2 = (f32[64,1024]{1,0:T(8,128)S(1)}, f32[64,1024]{1,0:T(8,128)}, u32[]{:S(2)}) copy-start(f32[64,1024]{1,0:T(8,128)} %get-tuple-element.11) | copy-start | bytes 786436
  91.1 3.9 %copy-start = (f32[27,128,32]{2,1,0:T(8,128)S(1)}, f32[27,128,32]{2,1,0:T(8,128)}, u32[]{:S(2)}) copy-start(f32[27,128,32]{2,1,0:T(8,128)} %get-tuple-element.17) | copy-start | bytes 1327108
  94.1 2.2 %copy-start.1 = (f32[1728,128]{1,0:T(8,128)S(1)}, f32[1728,128]{1,0:T(8,128)}, u32[]{:S(2)}) copy-start(f32[1728,128]{1,0:T(8,128)} %get-tuple-element.10) | copy-start | bytes 2654212

commit v6 on v5

--- a/solution.py
+++ b/solution.py
@@ -101,75 +101,71 @@
 
 
 class Summed:
-    def __init__(self, links, at, rows, whole, from_core, half, from_peers, total, from_filter, held):
-        self.links, self.at, self.rows = links, at, rows
-        self.whole, self.from_core, self.half, self.from_peers = whole, from_core, half, from_peers
-        self.total, self.from_filter, self.held = total, from_filter, held
-
-    def core(self):
+    def __init__(self, links, at, whole, rounded, arrived, column, split, split_in, ring, place, mine, ring_in, held):
+        self.links, self.at, self.whole, self.rounded, self.arrived = links, at, whole, rounded, arrived
+        self.column, self.split, self.split_in = column, split, split_in
+        self.ring, self.place, self.mine, self.ring_in, self.held = ring, place, mine, ring_in, held
+        self.rows, self.step = arrived.shape[1], mine.shape[0]
+
+    def scatter(self):
         ns, nf, nm, s, f, m = self.at
-        span = self.half.shape[0]
-        core = lax.rem(s, 2)
-        partner = {"spatial": s + 1 - 2 * core}
-        self.moving = [self.links(self.whole.at[pl.ds((1 - core) * span, span)], self.from_core, partner)]
+        self.rounded[...] = self.whole[...].astype(BF)
+        self.targets, self.moving = [], []
+        for r in range(1, ns):
+            j = lax.rem(s + r, ns)
+            self.targets.append({"spatial": j})
+            self.moving.append(
+                self.links(self.rounded.at[pl.ds(j * self.rows, self.rows)], self.arrived.at[r - 1], {"spatial": j})
+            )
         start(self.moving)
 
-    def peers(self):
-        ns, nf, nm, s, f, m = self.at
-        span, rows = self.half.shape[0], self.rows
-        core, count = lax.rem(s, 2), span // rows
-        me = (s // 2) * nm + m
+    def spatial_sum(self):
         wait(self.moving)
-        self.half[...] = self.whole[pl.ds(core * span, span)] + self.from_core[...]
-        self.targets = []
-        self.moving = []
-        for r in range(1, count):
-            j = lax.rem(me + r, count)
-            device = {"spatial": (j // nm) * 2 + core, "sample": lax.rem(j, nm)}
-            self.targets.append(device)
-            self.moving.append(self.links(self.half.at[pl.ds(j * rows, rows)], self.from_peers.at[r - 1], device))
-        start(self.moving)
-
-    def gather_sum(self):
-        ns, nf, nm, s, f, m = self.at
-        wait(self.moving)
-        value = self.half[pl.ds(((s // 2) * nm + m) * self.rows, self.rows)]
-        for r in range(len(self.moving)):
-            value = value + self.from_peers[r]
+        value = self.whole[pl.ds(self.at[3] * self.rows, self.rows)]
+        for r in range(len(self.targets)):
+            value = value + self.arrived[r].astype(F32)
         return value
 
-    def filters(self):
-        ns, nf, nm, s, f, m = self.at
-        value = self.gather_sum()
-        self.total[...] = value
-        self.from_filter[f] = value
+    def columns(self):
+        self.split[...] = self.spatial_sum()
         self.moving = [
-            self.links(self.total, self.from_filter.at[f], {"filter": lax.rem(f + r, nf)}) for r in range(1, nf)
+            self.links(self.split.at[pl.ds(y * self.step, self.step)], self.split_in.at[i], device)
+            for i, (y, device) in enumerate(self.column)
         ]
         start(self.moving)
 
-    def back(self):
-        ns, nf, nm, s, f, m = self.at
-        if self.from_filter is None:
-            value = self.gather_sum()
+    def rings(self):
+        if self.split is None:
+            value = self.spatial_sum()
         else:
             wait(self.moving)
-            value = self.from_filter[0]
-            for k in range(1, nf):
-                value = value + self.from_filter[k]
-        span, rows = self.half.shape[0], self.rows
-        self.base = pl.ds(lax.rem(s, 2) * span, span)
-        mine = pl.ds(lax.rem(s, 2) * span + ((s // 2) * nm + m) * rows, rows)
-        self.held[mine] = value.astype(BF)
-        self.moving = [self.links(self.held.at[mine], self.held.at[mine], device) for device in self.targets]
+            value = self.split[pl.ds(self.at[4] // 2 * self.step, self.step)]
+            for i in range(len(self.column)):
+                value = value + self.split_in[i]
+        self.mine[...] = value
+        self.ring_in[self.place] = value
+        self.moving = [self.links(self.mine, self.ring_in.at[self.place], device) for device in self.ring]
         start(self.moving)
 
-    def across(self):
-        s = self.at[3]
+    def back(self):
         wait(self.moving)
-        self.moving = [
-            self.links(self.held.at[self.base], self.held.at[self.base], {"spatial": s + 1 - 2 * lax.rem(s, 2)})
-        ]
+        value = self.ring_in[0]
+        for i in range(1, self.ring_in.shape[0]):
+            value = value + self.ring_in[i]
+        base = self.at[3] * self.rows
+        self.block = pl.ds(base, self.rows)
+        if self.split is not None:
+            here = pl.ds(base + self.at[4] // 2 * self.step, self.step)
+            self.held[here] = value.astype(BF)
+            self.moving = [self.links(self.held.at[here], self.held.at[here], device) for y, device in self.column]
+            start(self.moving)
+        else:
+            self.held[self.block] = value.astype(BF)
+            self.moving = []
+
+    def spread(self):
+        wait(self.moving)
+        self.moving = [self.links(self.held.at[self.block], self.held.at[self.block], device) for device in self.targets]
         start(self.moving)
 
     def finish(self):
@@ -206,15 +202,15 @@
 
 
 def whole_step(
-    scaling, vt, ct, wl, w1, mo, g2o, g1o, vg,
-    vs, vo, cx, cg, wg, v3, c3, x3, hs, pre, acc, w1t, w1v, wm, me, mr, bp, bh, b3, v3o, g2a,
-    g1w, g1c, g1h, g1p, g1t, g1f, g1b, g2w, g2c, g2h, g2p, g2b, send, recv,
+    scaling, vt, ct, wlt, w1, mo, g2o, g1o, vg,
+    vs, vo, cx, cg, cp, cy, wg, v3, c3, x3, hs, pre, acc, w1t, w1v, wm, me, mr, bp, bh, b3, v3o, wl,
+    g1w, g1s, g1p, g1q, g1y, g1m, g1r, g1b, g2w, g2s, g2p, g2m, g2r, g2b, send, recv,
 ):
     at = ns, nf, nm, s, f, m = places()
     links = Links(send, recv)
     depth, rows = DEPTH, 2 * nf
     wide = rows + 2
-    part = wl.shape[0] // ns
+    part = 128 // ns
     nz = ns // 2
     core, z = lax.rem(s, 2), s // 2
     down, up = lax.rem(s + ns - 1, ns), lax.rem(s + 1, ns)
@@ -226,21 +222,36 @@
         {"spatial": down, "filter": left}, {"spatial": down, "filter": right},
         {"spatial": up, "filter": left}, {"spatial": up, "filter": right},
     ]
-    group = []
-    for r in range(1, nz * nm):
-        j = lax.rem(z * nm + m + r, nz * nm)
-        group.append({"spatial": (j // nm) * 2 + core, "sample": lax.rem(j, nm)})
-    greet([{"filter": p} for p in peers] + edges[2:] + group)
+    ring = []
+    for i in range(1, 2 * nm):
+        j = lax.rem(lax.rem(f, 2) * nm + m + i, 2 * nm)
+        ring.append({"filter": f - lax.rem(f, 2) + j // nm, "sample": lax.rem(j, nm)})
+    other_sample = [{"sample": lax.rem(m + i, nm)} for i in range(1, nm)]
+    group = [{"spatial": lax.rem(s + r, ns)} for r in range(1, ns)] + ring
+    wl[...] = jnp.concatenate([wlt[...], jnp.zeros((32, 128), BF)], axis=0).T
+    greet([{"filter": p} for p in peers] + edges[4:] + group)
 
     inner, body, two, pair = pl.ds(1, depth), pl.ds(0, depth), pl.ds(0, 2), pl.ds(1, 2)
     block = pl.ds(1 + 2 * f, 2)
-    blocks = [links(vt, vs.at[inner, block], {"filter": p}) for p in peers]
+    ny = nf // 2
+    xl, yy = lax.rem(f, 2), f // 2
+    fx = f + 1 - 2 * xl
+    partner = {"filter": fx}
+    ys = [lax.rem(yy + r, ny) for r in range(1, ny)]
+    sources = [2 * lax.rem(yy + ny - r, ny) + xl for r in range(1, ny)]
+    column = [{"filter": 2 * y + xl} for y in ys]
+    lo, hi, glo, ghi = pl.ds(0, 2), pl.ds(2, 2), pl.ds(1, 2), pl.ds(3, 2)
+    vol_x = links(vt, vs.at[inner, block], partner)
+    vol_y = [links(vt, vs.at[inner, block], device) for device in column]
     mine = pl.ds(s * part, part)
     halo = [links(ct.at[0], cx.at[depth + 1], prev), links(ct.at[depth - 1], cx.at[0], after)]
     weights = [links(wl.at[mine], wg.at[f, mine], {"filter": p}) for p in peers]
-    cots = [links(ct.at[:, pl.ds(2 * p, 4)], cg.at[f, inner], {"filter": p}) for p in peers]
+    cot_x = links(ct.at[lo, pl.ds(2 - 2 * xl, rows)], cp, partner)
+    cot_y = [links(ct.at[hi, pl.ds(4 * y, 6)], cy.at[i], column[i]) for i, y in enumerate(ys)]
+    cots = [links(ct.at[hi, pl.ds(2 * fx, 4)], cg.at[f, ghi], partner)]
+    cots += [links(ct.at[lo, pl.ds(4 * y + 2 * xl, 4)], cg.at[f, glo], column[i]) for i, y in enumerate(ys)]
     corners = [links(src, dst, device) for (src, dst), device in zip(around(vt, vo), edges)]
-    for copies in (weights, halo, corners, cots):
+    for copies in (weights, [cot_x], cot_y, cots, corners, halo):
         start(copies)
 
     vs[:, 0] = jnp.zeros_like(vs[:, 0])
@@ -250,7 +261,6 @@
     cg[f, inner] = ct[:, pl.ds(2 * f, 4)]
     wg[f, mine] = wl[mine]
     w1t[...] = w1[...].T
-    wlt = wl[...].T
     for sx in range(3):
         for sy in range(3):
             for sz in range(3):
@@ -261,7 +271,7 @@
     zero(hs)
     zero(me)
     zero(acc)
-    zero(g2a)
+    zero(g2w)
 
     wait(weights)
     along = [
@@ -269,6 +279,20 @@
     ]
     start(along)
 
+    cot_x.wait()
+    onward = [links(cp.at[:, pl.ds(4 * y, 4)], cg.at[fx, glo], column[i]) for i, y in enumerate(ys)]
+    start(onward)
+    cots += onward
+    cg[fx, glo] = cp[:, pl.ds(4 * yy, 4)]
+    for i, k in enumerate(sources):
+        cot_y[i].wait()
+        onward = links(cy.at[i, :, pl.ds(2 - 2 * xl, 4)], cg.at[k, ghi], partner)
+        onward.start()
+        cots.append(onward)
+        cg[k, ghi] = cy[i, :, pl.ds(2 * xl, 4)]
+
+    start([vol_x] + vol_y)
+
     wait(halo)
 
     @pl.when(s == 0)
@@ -281,9 +305,6 @@
 
     cxr = cx.reshape((depth + 2) * wide, 32, 128)
     spread(cxr, x3, True)
-    for plane in (0, depth + 1):
-        cg[f, plane] = cx[plane, pl.ds(2 * f, 4)]
-
     wait(corners)
     vo[inner, pair] = vt[...]
     clear_outside(vo, at)
@@ -294,15 +315,9 @@
             w1t[...], columns(v3o, 4, OWN[4 * part_at : 4 * part_at + 4], False, 0), preferred_element_type=F32
         )
 
-    forward = []
-    for r, copy in enumerate(cots):
-        copy.wait()
-        k = lax.rem(f + nf - 1 - r, nf)
-        pieces = [links(cg.at[k, 1], cg.at[k, depth + 1], prev), links(cg.at[k, depth], cg.at[k, 0], after)]
-        start(pieces)
-        forward += pieces
-
-    start(blocks)
+    wait(cots)
+    forward = [links(cg.at[:, 1], cg.at[:, depth + 1], prev), links(cg.at[:, depth], cg.at[:, 0], after)]
+    start(forward)
     cgr = cg.reshape(nf, (depth + 2) * 4, 32, 128)
 
     def inside(k, carry):
@@ -310,6 +325,16 @@
         return carry
 
     lax.fori_loop(0, nf, inside, 0)
+    vol_x.wait()
+    over = pl.ds(1 + 2 * fx, 2)
+    blocks = [links(vs.at[glo, over], vs.at[glo, over], device) for device in column]
+    start(blocks)
+    for copy, k in zip(vol_y, sources):
+        copy.wait()
+        there = pl.ds(1 + 2 * k, 2)
+        onward = links(vs.at[ghi, there], vs.at[ghi, there], partner)
+        onward.start()
+        blocks.append(onward)
     wait(along)
     across = []
     for k in range(nz):
@@ -344,7 +369,6 @@
         sig = jax.nn.sigmoid(u)
         bp[x, y] = (acc[:, 128 * n : 128 * (n + 1)] * (sig * (1.0 + u * (1.0 - sig)))).astype(BF)
     cells = [links(src, dst, device) for (src, dst), device in zip(around(bp, bh), edges)]
-    start(cells)
     bh[inner, pair] = bp[...]
 
     grads = jnp.concatenate([bp[x, y] for x, y in OWN], axis=1)
@@ -353,8 +377,11 @@
         field = jnp.concatenate([v3o[(x + sx) * 4 + y + sy] for x, y in OWN], axis=1)
         g1w[192 * j : 192 * (j + 1)] = lax.dot_general(field, grads, NT, preferred_element_type=F32)
     g1w[1728:] = jnp.zeros((g1w.shape[0] - 1728, 128), F32)
-    one = Summed(links, at, g1t.shape[0], g1w, g1c, g1h, g1p, g1t, g1f, g1b)
-    one.core()
+    one = Summed(
+        links, at, g1w, g1s, g1p, list(zip(ys, column)), g1q, g1y, ring, xl * nm + m, g1m, g1r, g1b
+    )
+    one.scatter()
+    start(cells)
 
     wait(blocks)
     row = pl.ds(1, rows)
@@ -376,7 +403,6 @@
         return carry
 
     lax.fori_loop(times, 3 * times, first, 0)
-    one.peers()
     wait(planes)
 
     @pl.when(s == 0)
@@ -392,21 +418,21 @@
         spread(vsr.at[span], v3.at[span], False)
     lax.fori_loop(0, times, first, 0)
     lax.fori_loop(3 * times, 4 * times, first, 0)
-    one.filters()
+
+    one.columns()
 
     def second_weights(i, carry):
         x, y = i // times, lax.rem(i, times) * lot
         here = jnp.concatenate([hs[x * wide + y + j + 1] for j in range(lot)], axis=1)
         field = columns(x3, wide, [(x, y + j) for j in range(lot)], True, 32)
-        g2a[...] += lax.dot_general(here, field, NT, preferred_element_type=F32)
+        g2w[...] += lax.dot_general(field, here, NT, preferred_element_type=F32)
         return carry
 
-    lax.fori_loop(0, 4 * times, second_weights, 0)
-    for t in range(7):
-        g2w[128 * t : 128 * (t + 1)] = g2a[:, 128 * t : 128 * (t + 1)]
-    g2w[896:] = jnp.zeros((g2w.shape[0] - 896, 128), F32)
-    other = Summed(links, at, g2p.shape[1], g2w, g2c, g2h, g2p, None, None, g2b)
-    other.core()
+    lax.fori_loop(0, 2 * times, second_weights, 0)
+    one.rings()
+    lax.fori_loop(2 * times, 4 * times, second_weights, 0)
+    other = Summed(links, at, g2w, g2s, g2p, [], None, None, other_sample, m, g2m, g2r, g2b)
+    other.scatter()
     one.back()
 
     def second(i, carry):
@@ -432,15 +458,16 @@
 
     turn = rows // 4
     lax.fori_loop(0, 2 * turn, second, 0)
-    other.peers()
-    one.across()
+    one.spread()
+    other.rings()
     lax.fori_loop(2 * turn, 4 * turn, second, 0)
+    other.back()
+    other.spread()
     outer = [
         links(me.at[pl.ds(0, rows)], mr.at[1], prev),
         links(me.at[pl.ds((depth + 1) * rows, rows)], mr.at[0], after),
     ]
     start(outer)
-    other.back()
 
     wait(cells)
     clear_outside(bh, at)
@@ -450,24 +477,21 @@
         vg[:, lanes] = jnp.dot(
             w1v[...], columns(b3, 4, OWN[4 * part_at : 4 * part_at + 4], True, 0), preferred_element_type=F32
         )
-    other.across()
+    mo[...] = me[pl.ds(rows, depth * rows)]
+    wait(outer)
+
+    @pl.when(s > 0)
+    def _():
+        mo[pl.ds(0, rows)] += mr[0]
+
+    @pl.when(s < ns - 1)
+    def _():
+        mo[pl.ds((depth - 1) * rows, rows)] += mr[1]
+
+    other.finish()
+    g2o[...] = g2b[0:864].astype(F32) * scaling
     one.finish()
     g1o[...] = g1b[0:1728].astype(F32) * scaling
-    mo[...] = me[pl.ds(rows, depth * rows)]
-    wait(outer)
-
-    @pl.when(s > 0)
-    def _():
-        mo[pl.ds(0, rows)] += mr[0]
-
-    @pl.when(s < ns - 1)
-    def _():
-        mo[pl.ds((depth - 1) * rows, rows)] += mr[1]
-
-    other.finish()
-    for k in range(27):
-        tile = g2b[128 * (k // 4) : 128 * (k // 4 + 1)].astype(F32) * scaling
-        g2o[k] = tile[:, 32 * (k % 4) : 32 * (k % 4 + 1)]
 
 
 def on_device(volume, weight_first, weight_second, cotangent):
@@ -475,37 +499,36 @@
     depth, rows = DEPTH, 2 * nf
     wide = rows + 2
     scaling = 1.0 / math.sqrt(nm * depth * ns * rows * 128)
-    count = ns // 2 * nm
 
     vt = volume[0].transpose(1, 2, 0, 3)
     ct = jnp.pad(cotangent[0].transpose(1, 2, 0, 3), ((0, 0), (1, 1), (0, 0), (0, 0)))
-    wl = jnp.pad(weight_second.transpose(1, 0, 2).reshape(128, 864), ((0, 0), (0, 32)))
+    wlt = weight_second.transpose(0, 2, 1).reshape(864, 128)
     w1 = weight_first.reshape(1728, 128)
 
-    len1 = -(-1728 // (32 * count)) * 16
-    len2 = -(-1024 // (32 * count)) * 16
+    columns_of = nf // 2
+    step1 = -(-1728 // (16 * ns * columns_of)) * 16
+    len1, len2 = step1 * columns_of, 896 // ns
     slab = (depth + 2) * wide
     scratch = [
         ((depth + 2, wide, 64, 128), BF), ((depth + 2, 4, 64, 128), BF), ((depth + 2, wide, 32, 128), BF),
-        ((nf, depth + 2, 4, 32, 128), BF), ((nf, 128, 896), BF),
+        ((nf, depth + 2, 4, 32, 128), BF), ((2, rows, 32, 128), BF), ((max(nf // 2 - 1, 1), 2, 6, 32, 128), BF), ((nf, 128, 896), BF),
         ((slab, 192, 128), BF), ((nf, 24, 96, 128), BF), ((slab, 96, 128), BF),
         ((depth * wide, 128, 128), BF), ((128, 1024), F32), ((128, 1024), F32),
         ((128, 1728), BF), ((64, 3456), BF), ((288, 384), BF),
         (((depth + 2) * rows, 32, 128), F32), ((2, rows, 32, 128), F32),
         ((depth, 2, 128, 128), BF), ((depth + 2, 4, 128, 128), BF), ((24, 384, 128), BF),
-        ((24, 192, 128), BF), ((128, 896), F32),
-        ((2 * count * len1, 128), F32), ((count * len1, 128), F32), ((count * len1, 128), F32),
-        ((count - 1, len1, 128), F32), ((len1, 128), F32), ((nf, len1, 128), F32),
-        ((2 * count * len1, 128), BF),
-        ((2 * count * len2, 128), F32), ((count * len2, 128), F32), ((count * len2, 128), F32),
-        ((count - 1, len2, 128), F32), ((2 * count * len2, 128), BF),
+        ((24, 192, 128), BF), ((128, 896), BF),
+        ((ns * len1, 128), F32), ((ns * len1, 128), BF), ((ns - 1, len1, 128), BF), ((len1, 128), F32),
+        ((max(columns_of - 1, 1), step1, 128), F32), ((step1, 128), F32), ((2 * nm, step1, 128), F32), ((ns * len1, 128), BF),
+        ((ns * len2, 128), F32), ((ns * len2, 128), BF), ((ns - 1, len2, 128), BF),
+        ((len2, 128), F32), ((nm, len2, 128), F32), ((ns * len2, 128), BF),
     ]
-    copies = 128
+    copies = 160
     mo, g2o, g1o, vg = pl.pallas_call(
         functools.partial(whole_step, scaling),
         out_shape=[
             jax.ShapeDtypeStruct((depth * rows, 32, 128), F32),
-            jax.ShapeDtypeStruct((27, 128, 32), F32),
+            jax.ShapeDtypeStruct((864, 128), F32),
             jax.ShapeDtypeStruct((1728, 128), F32),
             jax.ShapeDtypeStruct((64, 1024), F32),
         ],
@@ -515,9 +538,9 @@
         compiler_params=pltpu.CompilerParams(
             vmem_limit_bytes=LIMIT, collective_id=0, has_side_effects=True
         ),
-    )(vt, ct, wl, w1)
+    )(vt, ct, wlt, w1)
     mapped = mo.reshape(depth, rows, 32, 128).transpose(2, 0, 1, 3)[None]
-    return (mapped, g2o, g1o.reshape(27, 64, 128), vg.reshape(1, 64, depth, 2, 128))
+    return (mapped, g2o.reshape(27, 32, 128).transpose(0, 2, 1), g1o.reshape(27, 64, 128), vg.reshape(1, 64, depth, 2, 128))
 
 
 def solution(mesh):

time: 97.4 us -> 93.8 us (0.963); the launches traced: 97.2 us -> 92.4 us
  local copies, waits for them, and re-layouts: 11.7 us -> 9.3 us
  Pallas kernels: 84.8 us -> 82.5 us
    pallas_call x1, Pallas kernels: 84.8 us -> 82.5 us  [on_device(): pl.pallas_call(functools.partial(whole_step, scaling), out_shape=[jax.Sha...]
    reshape x1 -> x0, local copies, waits for them, and re-layouts: 1.09 us -> none  [on_device(): weight_second.transpose(1, 0, 2).reshape(128, 864)]
where the time goes in v6:
time: 93.8 us; the launch traced here: 92.4 us
  Pallas kernels  82.5 us (88%)
  local copies, waits for them, and re-layouts  9.3 us (10%)
    pallas_call x1, Pallas kernels, on_device(): pl.pallas_call(functools.partial(whole_step, scaling), out_shape=[jax.Sha...  82.5 us
    unnamed x10, local copies, waits for them, and re-layouts  4.65 us
    reshape x1, local copies, waits for them, and re-layouts, on_device(): mapped = mo.reshape(depth, rows, 32, 128).transpose(2, 0, 1, 3)[None]  2.87 us

profile of v6, /device:TPU:1, one launch (start us, length us, event | category | flops | bytes accessed | tf_op | source)
XLA Modules:
  0.0 92.4 jit_solution(10307854531089305479)
XLA Ops:
  0.6 1.6 %copy.16 = bf16[1,64,4,2,128]{4,1,3,2,0:T(8,128)(2,1)} copy(bf16[1,64,4,2,128]{4,3,2,1,0:T(2,128)(2,1)} %param.4) | data formatting | bytes 262144 | tf_op args[0]
  2.2 1.4 %copy.15 = bf16[1,32,4,16,128]{4,1,3,2,0:T(8,128)(2,1)S(1)} copy(bf16[1,32,4,16,128]{4,3,2,1,0:T(8,128)(2,1)} %param.7) | data formatting | bytes 1048576 | tf_op args[3]
  3.6 0.9 pad.4.ct
  4.5 82.5 %shard_map.75 = (f32[64,32,128]{2,1,0:T(8,128)}, f32[864,128]{1,0:T(8,128)}, f32[1728,128]{1,0:T(8,128)}, f32[64,1024]{1,0:T(8,128)}) custom-call(bf16[4,2,64,128]{3,2,1,0:T(8,128)(2,1)} %bitcast.28, bf16[4,18,32,128]{3,2,1,0:T(8,128)(2,1)} %pad.4.ct, bf16[864,128]{1,0:T(8,128)(2,1)} %bitcast.31, bf16[1728,128]{1,0:T(8,128)(2,1)} %bitcast.30), custom_call_target="tpu_custom_call" | custom-call | tf_op jit(solution)/shard_map/pallas_call | solution.py:527
  86.9 0.0 copy-start.2
  87.0 0.0 copy-start.1
  87.0 2.9 %copy.14 = f32[4,16,32,128]{3,1,0,2:T(8,128)} copy(f32[4,16,32,128]{3,2,1,0:T(8,128)} %bitcast.26) | data formatting | bytes 2097152 | tf_op jit(solution)/shard_map/reshape | solution.py:542
  89.8 0.0 copy-start
  89.8 0.0 copy-done.2
  89.8 0.9 reshape.31
  90.8 0.0 copy-done.1
  90.8 0.8 copy.19
  91.5 0.0 copy-done
  91.5 0.9 copy.20
Async XLA Ops:
  86.9 2.9 %copy-start.2 = (f32[64,1024]{1,0:T(8,128)S(1)}, f32[64,1024]{1,0:T(8,128)}, u32[]{:S(2)}) copy-start(f32[64,1024]{1,0:T(8,128)} %get-tuple-element.11) | copy-start | bytes 786436
  87.0 3.8 %copy-start.1 = (f32[864,128]{1,0:T(8,128)S(1)}, f32[864,128]{1,0:T(8,128)}, u32[]{:S(2)}) copy-start(f32[864,128]{1,0:T(8,128)} %get-tuple-element.9) | copy-start | bytes 1327108
  89.8 1.7 %copy-start = (f32[1728,128]{1,0:T(8,128)S(1)}, f32[1728,128]{1,0:T(8,128)}, u32[]{:S(2)}) copy-start(f32[1728,128]{1,0:T(8,128)} %get-tuple-element.10) | copy-start | bytes 2654212

commit v7 on v6

--- a/solution.py
+++ b/solution.py
@@ -352,6 +352,10 @@
     def _():
         cg[:, depth + 1] = jnp.zeros_like(cg[:, 0])
 
+    wait(blocks)
+    row = pl.ds(1, rows)
+    planes = [links(vs.at[1, row], vs.at[depth + 1, row], prev), links(vs.at[depth, row], vs.at[0, row], after)]
+    start(planes)
     def back(k, carry):
         for plane in (0, depth + 1):
             span = pl.ds(4 * plane, 4)
@@ -383,10 +387,6 @@
     one.scatter()
     start(cells)
 
-    wait(blocks)
-    row = pl.ds(1, rows)
-    planes = [links(vs.at[1, row], vs.at[depth + 1, row], prev), links(vs.at[depth, row], vs.at[0, row], after)]
-    start(planes)
     vsr = vs.reshape((depth + 2) * wide, 64, 128)
     spread(vsr.at[pl.ds(wide, depth * wide)], v3.at[pl.ds(wide, depth * wide)], False)
     lot = min(8, rows)

time: 93.8 us -> 89.6 us (0.955); the launches traced: 92.4 us -> 89.3 us
  Pallas kernels: 82.5 us -> 79.4 us
    pallas_call x1, Pallas kernels: 82.5 us -> 79.4 us  [on_device(): pl.pallas_call(functools.partial(whole_step, scaling), out_shape=[jax.Sha...]
where the time goes in v7:
time: 89.6 us; the launch traced here: 89.3 us
  Pallas kernels  79.4 us (89%)
  local copies, waits for them, and re-layouts  9.3 us (10%)
    pallas_call x1, Pallas kernels, on_device(): pl.pallas_call(functools.partial(whole_step, scaling), out_shape=[jax.Sha...  79.4 us
    unnamed x10, local copies, waits for them, and re-layouts  4.65 us
    reshape x1, local copies, waits for them, and re-layouts, on_device(): mapped = mo.reshape(depth, rows, 32, 128).transpose(2, 0, 1, 3)[None]  2.87 us

profile of v7, /device:TPU:1, one launch (start us, length us, event | category | flops | bytes accessed | tf_op | source)
XLA Modules:
  0.0 89.3 jit_solution(10312244408376021874)
XLA Ops:
  0.6 1.6 %copy.16 = bf16[1,64,4,2,128]{4,1,3,2,0:T(8,128)(2,1)} copy(bf16[1,64,4,2,128]{4,3,2,1,0:T(2,128)(2,1)} %param.4) | data formatting | bytes 262144 | tf_op args[0]
  2.2 1.4 %copy.15 = bf16[1,32,4,16,128]{4,1,3,2,0:T(8,128)(2,1)S(1)} copy(bf16[1,32,4,16,128]{4,3,2,1,0:T(8,128)(2,1)} %param.7) | data formatting | bytes 1048576 | tf_op args[3]
  3.6 0.9 pad.4.ct
  4.5 79.4 %shard_map.75 = (f32[64,32,128]{2,1,0:T(8,128)}, f32[864,128]{1,0:T(8,128)}, f32[1728,128]{1,0:T(8,128)}, f32[64,1024]{1,0:T(8,128)}) custom-call(bf16[4,2,64,128]{3,2,1,0:T(8,128)(2,1)} %bitcast.28, bf16[4,18,32,128]{3,2,1,0:T(8,128)(2,1)} %pad.4.ct, bf16[864,128]{1,0:T(8,128)(2,1)} %bitcast.31, bf16[1728,128]{1,0:T(8,128)(2,1)} %bitcast.30), custom_call_target="tpu_custom_call" | custom-call | tf_op jit(solution)/shard_map/pallas_call | solution.py:527
  83.9 0.0 copy-start.2
  83.9 0.0 copy-start.1
  83.9 2.9 %copy.14 = f32[4,16,32,128]{3,1,0,2:T(8,128)} copy(f32[4,16,32,128]{3,2,1,0:T(8,128)} %bitcast.26) | data formatting | bytes 2097152 | tf_op jit(solution)/shard_map/reshape | solution.py:542
  86.7 0.0 copy-start
  86.7 0.0 copy-done.2
  86.7 0.9 %reshape.31 = f32[1,64,4,2,128]{4,3,2,1,0:T(2,128)} reshape(f32[64,1024]{1,0:T(8,128)S(1)} %copy-done.2) | data formatting | bytes 524288 | tf_op jit(solution)/shard_map/reshape | solution.py:543
  87.7 0.0 copy-done.1
  87.7 0.8 copy.19
  88.4 0.0 copy-done
  88.4 0.9 %copy.20 = f32[27,64,128]{2,1,0:T(8,128)} copy(f32[27,64,128]{2,1,0:T(8,128)S(1)} %bitcast.27) | data formatting | bytes 1769472
Async XLA Ops:
  83.9 2.9 %copy-start.2 = (f32[64,1024]{1,0:T(8,128)S(1)}, f32[64,1024]{1,0:T(8,128)}, u32[]{:S(2)}) copy-start(f32[64,1024]{1,0:T(8,128)} %get-tuple-element.11) | copy-start | bytes 786436
  83.9 3.8 %copy-start.1 = (f32[864,128]{1,0:T(8,128)S(1)}, f32[864,128]{1,0:T(8,128)}, u32[]{:S(2)}) copy-start(f32[864,128]{1,0:T(8,128)} %get-tuple-element.9) | copy-start | bytes 1327108
  86.7 1.7 %copy-start = (f32[1728,128]{1,0:T(8,128)S(1)}, f32[1728,128]{1,0:T(8,128)}, u32[]{:S(2)}) copy-start(f32[1728,128]{1,0:T(8,128)} %get-tuple-element.10) | copy-start | bytes 2654212

commit v8 on v7

--- a/solution.py
+++ b/solution.py
@@ -202,8 +202,8 @@
 
 
 def whole_step(
-    scaling, vt, ct, wlt, w1, mo, g2o, g1o, vg,
-    vs, vo, cx, cg, cp, cy, wg, v3, c3, x3, hs, pre, acc, w1t, w1v, wm, me, mr, bp, bh, b3, v3o, wl,
+    scaling, vtr, ctr, wlt, w1, mo, g2o, g1o, vg,
+    vs, vo, cx, cg, cp, cy, wg, v3, c3, x3, hs, pre, acc, w1t, w1v, wm, me, mr, bp, bh, b3, v3o, wl, vt,
     g1w, g1s, g1p, g1q, g1y, g1m, g1r, g1b, g2w, g2s, g2p, g2m, g2r, g2b, send, recv,
 ):
     at = ns, nf, nm, s, f, m = places()
@@ -228,6 +228,12 @@
         ring.append({"filter": f - lax.rem(f, 2) + j // nm, "sample": lax.rem(j, nm)})
     other_sample = [{"sample": lax.rem(m + i, nm)} for i in range(1, nm)]
     group = [{"spatial": lax.rem(s + r, ns)} for r in range(1, ns)] + ring
+    cx[:, 0] = jnp.zeros_like(cx[:, 0])
+    cx[:, 2 * nf + 1] = jnp.zeros_like(cx[:, 0])
+    for x in range(DEPTH):
+        cx[x + 1, pl.ds(1, 2 * nf)] = jnp.swapaxes(ctr[:, pl.ds(x * 2 * nf, 2 * nf)].astype(F32), 0, 1).astype(BF)
+    ct = cx.at[pl.ds(1, DEPTH)]
+    vt[...] = jnp.swapaxes(vtr[...].astype(F32), 0, 1).astype(BF).reshape(DEPTH, 2, 64, 128)
     wl[...] = jnp.concatenate([wlt[...], jnp.zeros((32, 128), BF)], axis=0).T
     greet([{"filter": p} for p in peers] + edges[4:] + group)
 
@@ -244,7 +250,8 @@
     vol_x = links(vt, vs.at[inner, block], partner)
     vol_y = [links(vt, vs.at[inner, block], device) for device in column]
     mine = pl.ds(s * part, part)
-    halo = [links(ct.at[0], cx.at[depth + 1], prev), links(ct.at[depth - 1], cx.at[0], after)]
+    row = pl.ds(1, rows)
+    halo = [links(ct.at[0, row], cx.at[depth + 1, row], prev), links(ct.at[depth - 1, row], cx.at[0, row], after)]
     weights = [links(wl.at[mine], wg.at[f, mine], {"filter": p}) for p in peers]
     cot_x = links(ct.at[lo, pl.ds(2 - 2 * xl, rows)], cp, partner)
     cot_y = [links(ct.at[hi, pl.ds(4 * y, 6)], cy.at[i], column[i]) for i, y in enumerate(ys)]
@@ -257,7 +264,6 @@
     vs[:, 0] = jnp.zeros_like(vs[:, 0])
     vs[:, rows + 1] = jnp.zeros_like(vs[:, 0])
     vs[inner, block] = vt[...]
-    cx[inner] = ct[...]
     cg[f, inner] = ct[:, pl.ds(2 * f, 4)]
     wg[f, mine] = wl[mine]
     w1t[...] = w1[...].T
@@ -473,21 +479,23 @@
     clear_outside(bh, at)
     spread(bh.reshape((depth + 2) * 4, 128, 128), b3, True)
     for part_at in range(2):
-        lanes = pl.ds(512 * part_at, 512)
-        vg[:, lanes] = jnp.dot(
+        value = jnp.dot(
             w1v[...], columns(b3, 4, OWN[4 * part_at : 4 * part_at + 4], True, 0), preferred_element_type=F32
         )
-    mo[...] = me[pl.ds(rows, depth * rows)]
+        for j in range(4):
+            vg[:, 4 * part_at + j] = value[:, 128 * j : 128 * (j + 1)]
     wait(outer)
 
     @pl.when(s > 0)
     def _():
-        mo[pl.ds(0, rows)] += mr[0]
+        me[pl.ds(rows, rows)] += mr[0]
 
     @pl.when(s < ns - 1)
     def _():
-        mo[pl.ds((depth - 1) * rows, rows)] += mr[1]
-
+        me[pl.ds(depth * rows, rows)] += mr[1]
+
+    for x in range(depth):
+        mo[:, pl.ds(x * rows, rows)] = jnp.swapaxes(me[pl.ds((x + 1) * rows, rows)], 0, 1)
     other.finish()
     g2o[...] = g2b[0:864].astype(F32) * scaling
     one.finish()
@@ -500,8 +508,8 @@
     wide = rows + 2
     scaling = 1.0 / math.sqrt(nm * depth * ns * rows * 128)
 
-    vt = volume[0].transpose(1, 2, 0, 3)
-    ct = jnp.pad(cotangent[0].transpose(1, 2, 0, 3), ((0, 0), (1, 1), (0, 0), (0, 0)))
+    vt = volume.reshape(64, 2 * depth, 128)
+    ct = cotangent.reshape(32, depth * rows, 128)
     wlt = weight_second.transpose(0, 2, 1).reshape(864, 128)
     w1 = weight_first.reshape(1728, 128)
 
@@ -517,7 +525,7 @@
         ((128, 1728), BF), ((64, 3456), BF), ((288, 384), BF),
         (((depth + 2) * rows, 32, 128), F32), ((2, rows, 32, 128), F32),
         ((depth, 2, 128, 128), BF), ((depth + 2, 4, 128, 128), BF), ((24, 384, 128), BF),
-        ((24, 192, 128), BF), ((128, 896), BF),
+        ((24, 192, 128), BF), ((128, 896), BF), ((depth, 2, 64, 128), BF),
         ((ns * len1, 128), F32), ((ns * len1, 128), BF), ((ns - 1, len1, 128), BF), ((len1, 128), F32),
         ((max(columns_of - 1, 1), step1, 128), F32), ((step1, 128), F32), ((2 * nm, step1, 128), F32), ((ns * len1, 128), BF),
         ((ns * len2, 128), F32), ((ns * len2, 128), BF), ((ns - 1, len2, 128), BF),
@@ -527,10 +535,10 @@
     mo, g2o, g1o, vg = pl.pallas_call(
         functools.partial(whole_step, scaling),
         out_shape=[
-            jax.ShapeDtypeStruct((depth * rows, 32, 128), F32),
+            jax.ShapeDtypeStruct((32, depth * rows, 128), F32),
             jax.ShapeDtypeStruct((864, 128), F32),
             jax.ShapeDtypeStruct((1728, 128), F32),
-            jax.ShapeDtypeStruct((64, 1024), F32),
+            jax.ShapeDtypeStruct((64, 2 * depth, 128), F32),
         ],
         in_specs=[VMEM] * 4,
         out_specs=[VMEM] * 4,
@@ -539,7 +547,7 @@
             vmem_limit_bytes=LIMIT, collective_id=0, has_side_effects=True
         ),
     )(vt, ct, wlt, w1)
-    mapped = mo.reshape(depth, rows, 32, 128).transpose(2, 0, 1, 3)[None]
+    mapped = mo.reshape(1, 32, depth, rows, 128)
     return (mapped, g2o.reshape(27, 32, 128).transpose(0, 2, 1), g1o.reshape(27, 64, 128), vg.reshape(1, 64, depth, 2, 128))
 
 

time: 89.6 us -> 86.3 us (0.963)
  local copies, waits for them, and re-layouts: 9.3 us -> 5.48 us
    reshape x2 -> x0, local copies, waits for them, and re-layouts: 3.79 us -> none  [the longest x1 2.87 us: on_device(): mapped = mo.reshape(depth, rows, 32, 128).transpose(2, 0, 1, 3)[None]]
where the time goes in v8:
time: 86.3 us; the launch traced here: 86 us
  Pallas kernels  79.9 us (93%)
  local copies, waits for them, and re-layouts  5.48 us (6%)
    pallas_call x1, Pallas kernels, on_device(): pl.pallas_call(functools.partial(whole_step, scaling), out_shape=[jax.Sha...  79.9 us
    unnamed x10, local copies, waits for them, and re-layouts  5.48 us

profile of v8, /device:TPU:1, one launch (start us, length us, event | category | flops | bytes accessed | tf_op | source)
XLA Modules:
  0.0 86.0 jit_solution(14651949688748836943)
XLA Ops:
  0.6 79.9 %shard_map.75 = (f32[32,64,128]{2,1,0:T(8,128)}, f32[864,128]{1,0:T(8,128)}, f32[1728,128]{1,0:T(8,128)}, f32[64,8,128]{2,1,0:T(8,128)}) custom-call(bf16[64,8,128]{2,1,0:T(8,128)(2,1)} %bitcast.19, bf16[32,64,128]{2,1,0:T(8,128)(2,1)} %bitcast.14, bf16[864,128]{1,0:T(8,128)(2,1)} %bitcast.18, bf16[1728,128]{1,0:T(8,128)(2,1)} %bitcast.15), custom_call_target="tpu_custom_call" | custom-call | tf_op jit(solution)/shard_map/pallas_call | solution.py:535
  80.5 0.0 copy-start.1
  80.5 2.4 %copy.12 = f32[1,32,4,16,128]{4,3,2,1,0:T(8,128)} copy(f32[1,32,4,16,128]{4,3,2,1,0:T(8,128)} %bitcast.12) | data formatting | bytes 2097152
  82.9 0.0 copy-done.1
  82.9 0.0 copy-start
  82.9 0.8 copy.13
  83.7 0.6 copy-done
  84.2 0.0 copy-start.2
  84.2 0.9 %copy.14 = f32[27,64,128]{2,1,0:T(8,128)} copy(f32[27,64,128]{2,1,0:T(8,128)S(1)} %bitcast.13) | data formatting | bytes 1769472
  85.1 0.2 copy-done.2
  85.3 0.7 copy.15
Async XLA Ops:
  80.5 2.4 %copy-start.1 = (f32[864,128]{1,0:T(8,128)S(1)}, f32[864,128]{1,0:T(8,128)}, u32[]{:S(2)}) copy-start(f32[864,128]{1,0:T(8,128)} %get-tuple-element.9) | copy-start | bytes 1327108
  82.9 1.3 %copy-start = (f32[1728,128]{1,0:T(8,128)S(1)}, f32[1728,128]{1,0:T(8,128)}, u32[]{:S(2)}) copy-start(f32[1728,128]{1,0:T(8,128)} %get-tuple-element.10) | copy-start | bytes 2654212
  84.2 1.1 %copy-start.2 = (f32[64,8,128]{2,1,0:T(8,128)S(1)}, f32[64,8,128]{2,1,0:T(8,128)}, u32[]{:S(2)}) copy-start(f32[64,8,128]{2,1,0:T(8,128)} %get-tuple-element.11) | copy-start | bytes 786436

commit v9 on v8

--- a/solution.py
+++ b/solution.py
@@ -535,10 +535,10 @@
     mo, g2o, g1o, vg = pl.pallas_call(
         functools.partial(whole_step, scaling),
         out_shape=[
-            jax.ShapeDtypeStruct((32, depth * rows, 128), F32),
-            jax.ShapeDtypeStruct((864, 128), F32),
-            jax.ShapeDtypeStruct((1728, 128), F32),
-            jax.ShapeDtypeStruct((64, 2 * depth, 128), F32),
+            pltpu.VMEM((32, depth * rows, 128), F32),
+            pltpu.VMEM((864, 128), F32),
+            pltpu.VMEM((1728, 128), F32),
+            pltpu.VMEM((64, 2 * depth, 128), F32),
         ],
         in_specs=[VMEM] * 4,
         out_specs=[VMEM] * 4,

time: 86.3 us -> 82.6 us (0.957)
  local copies, waits for them, and re-layouts: 5.48 us -> 3.35 us
  Pallas kernels: 79.9 us -> 78.5 us
    unnamed x10 -> x4, local copies, waits for them, and re-layouts: 5.48 us -> 3.35 us
    pallas_call x1, Pallas kernels: 79.9 us -> 78.5 us  [on_device(): pl.pallas_call(functools.partial(whole_step, scaling), out_shape=[pltpu.V...]
where the time goes in v9:
time: 82.6 us; the launch traced here: 82.4 us
  Pallas kernels  78.5 us (95%)
  local copies, waits for them, and re-layouts  3.35 us (4%)
    pallas_call x1, Pallas kernels, on_device(): pl.pallas_call(functools.partial(whole_step, scaling), out_shape=[pltpu.V...  78.5 us
    unnamed x4, local copies, waits for them, and re-layouts  3.35 us

profile of v9, /device:TPU:1, one launch (start us, length us, event | category | flops | bytes accessed | tf_op | source)
XLA Modules:
  0.0 82.4 jit_solution(6873537087182121569)
XLA Ops:
  0.6 78.5 %shard_map.75 = (f32[32,64,128]{2,1,0:T(8,128)S(1)}, f32[864,128]{1,0:T(8,128)S(1)}, f32[1728,128]{1,0:T(8,128)S(1)}, f32[64,8,128]{2,1,0:T(8,128)S(1)}) custom-call(bf16[64,8,128]{2,1,0:T(8,128)(2,1)} %bitcast.19, bf16[32,64,128]{2,1,0:T(8,128)(2,1)} %bitcast.16, bf16[864,128]{1,0:T(8,128)(2,1)} %bitcast.18, bf16[1728,128]{1,0:T(8,128)(2,1)} %bitcast.17), custom_call_target="tpu_custom_call" | custom-call | tf_op jit(solution)/shard_map/pallas_call | solution.py:535
  79.1 1.0 %copy.12 = f32[1,32,4,16,128]{4,3,2,1,0:T(8,128)} copy(f32[1,32,4,16,128]{4,3,2,1,0:T(8,128)S(1)} %bitcast.12) | data formatting | bytes 2097152
  80.1 0.8 copy.13
  80.8 0.7 copy.15
  81.5 0.9 %copy.14 = f32[27,64,128]{2,1,0:T(8,128)} copy(f32[27,64,128]{2,1,0:T(8,128)S(1)} %bitcast.13) | data formatting | bytes 1769472

commit v10 on v9

--- a/solution.py
+++ b/solution.py
@@ -442,15 +442,15 @@
     one.back()
 
     def second(i, carry):
-        x, y = i // (rows // 4), lax.rem(i, rows // 4) * 4
+        x, y = i // (times), lax.rem(i, times) * lot
         field = jnp.concatenate(
-            [jnp.concatenate([hs[x * wide + y + j + sy] for j in range(4)], axis=1) for sy in range(3)],
+            [jnp.concatenate([hs[x * wide + y + j + sy] for j in range(lot)], axis=1) for sy in range(3)],
             axis=0,
         )
         value = jnp.dot(wm[...], field, preferred_element_type=F32)
         lane = lax.broadcasted_iota(jnp.int32, (32, 128), 1)
         for sx in range(3):
-            for j in range(4):
+            for j in range(lot):
                 lanes = slice(128 * j, 128 * (j + 1))
                 base = 96 * sx
                 below = pltpu.roll(value[base : base + 32, lanes], 1, 1)
@@ -462,7 +462,7 @@
                 )
         return carry
 
-    turn = rows // 4
+    turn = times
     lax.fori_loop(0, 2 * turn, second, 0)
     one.spread()
     other.rings()

time: 82.6 us -> 82.6 us (level)
  no operation moved by 1% of the time
where the time goes in v10:
time: 82.6 us; the launch traced here: 82.4 us
  Pallas kernels  78.5 us (95%)
  local copies, waits for them, and re-layouts  3.35 us (4%)
    pallas_call x1, Pallas kernels, on_device(): pl.pallas_call(functools.partial(whole_step, scaling), out_shape=[pltpu.V...  78.5 us
    unnamed x4, local copies, waits for them, and re-layouts  3.35 us

profile of v10, /device:TPU:1, one launch (start us, length us, event | category | flops | bytes accessed | tf_op | source)
XLA Modules:
  0.0 82.4 jit_solution(9933360422252560924)
XLA Ops:
  0.6 78.5 %shard_map.75 = (f32[32,64,128]{2,1,0:T(8,128)S(1)}, f32[864,128]{1,0:T(8,128)S(1)}, f32[1728,128]{1,0:T(8,128)S(1)}, f32[64,8,128]{2,1,0:T(8,128)S(1)}) custom-call(bf16[64,8,128]{2,1,0:T(8,128)(2,1)} %bitcast.19, bf16[32,64,128]{2,1,0:T(8,128)(2,1)} %bitcast.16, bf16[864,128]{1,0:T(8,128)(2,1)} %bitcast.18, bf16[1728,128]{1,0:T(8,128)(2,1)} %bitcast.17), custom_call_target="tpu_custom_call" | custom-call | tf_op jit(solution)/shard_map/pallas_call | solution.py:535
  79.1 1.0 %copy.12 = f32[1,32,4,16,128]{4,3,2,1,0:T(8,128)} copy(f32[1,32,4,16,128]{4,3,2,1,0:T(8,128)S(1)} %bitcast.12) | data formatting | bytes 2097152
  80.1 0.8 copy.13
  80.8 0.7 copy.15
  81.5 0.9 %copy.14 = f32[27,64,128]{2,1,0:T(8,128)} copy(f32[27,64,128]{2,1,0:T(8,128)S(1)} %bitcast.13) | data formatting | bytes 1769472
